TPU v7x, 512 devices: a whole 4x4x16 slice. The times are simulated.
512 devices in a mesh: tm: 8 (over z_hi, y), mesh: 64 (over z_lo, x, core).
Axes of the slice: x: 4, y: 4, z: 16 (z_hi: 2, z_lo: 8; z = z_hi * 8 + z_lo), core: 2. Of those that a mesh axis runs over, the one named last changes fastest.
Arguments:
- inverse: bfloat16 [8, 135, 135, 8192], P('tm', None, None, 'mesh'), may hold values from -0.3 to 1.9
- start: float32 [8, 135, 8192], P('tm', None, 'mesh'), may hold values from -6 to 6
- source: float32 [8, 135, 8192], P('tm', None, 'mesh'), may hold values from -6 to 6
- mass: float32 [135, 8192], P(None, 'mesh'), may hold values from 0.1 to 1
- inner_elem: int32 [2, 16384], P(None, 'mesh'), may hold values from 0 to 127
- inner_face: int32 [2, 16384], P(None, 'mesh'), may hold values from 0 to 5
- inner_orient: int32 [16384], P('mesh'), may hold values from 0 to 7
- inner_jac: float32 [8, 2, 25, 16384], P('tm', None, None, 'mesh'), may hold values from -0.72 to 0.72
- cross_elem: int32 [64, 160], P('mesh'), may hold values from 0 to 127
- cross_face: int32 [64, 160], P('mesh'), may hold values from 0 to 5
- cross_orient: int32 [64, 160], P('mesh'), may hold values from 0 to 7, as said below
- cross_count: int32 [64, 5], P('mesh'), may hold values from 1 to 32, as said below
- cross_jac: float32 [8, 25, 64, 160], P('tm', None, 'mesh'), may hold values from -0.72 to 0.72
Outputs:
- adjoint: float32 [8, 135, 8192], P('tm', None, 'mesh')
Inputs may be any that keep to these rules, and one draw needn't show every extreme that they name: cross_count[(p + off[k]) mod 64, mirror[k]] = cross_count[p, k], and cross_count[p, 3] = 32. cross_orient[(p + off[k]) mod 64, mirror[k] * 32 + s] = inv(cross_orient[p, k * 32 + s]).
All inputs are finite; a program needn't handle non-finite values.
Results may differ from a plain program's by a relative error of at most 0.008.
Values sent between devices are 32-bit elements; how exact they have to be, the bound alone decides.
No kernel may reach another device: no remote copies, remote signals or barrier semaphores. Data moves between devices by JAX's collectives and lax.ppermute only.
A program may use at most 128 MiB of HBM per device.

v0:
```python
import math

import jax
import jax.numpy as jnp
import numpy as np
from jax import lax
from jax.sharding import PartitionSpec as P

SWEEPS = 2


line_weights = (1.0 / 3.0, 4.0 / 3.0, 1.0 / 3.0)
highest = lax.Precision.HIGHEST
mirror_list = (1, 0, 4, 3, 2)


def build_tables():
    face_nodes = np.zeros((6, 9), np.int32)
    face_weight = np.zeros((9,), np.float32)
    for face_index in range(6):
        normal_axis = face_index // 2
        tangent_axes = [other_axis for other_axis in range(3) if other_axis != normal_axis]
        for tangent_v in range(3):
            for tangent_u in range(3):
                coords = [0, 0, 0]
                coords[normal_axis] = 2 * (face_index % 2)
                coords[tangent_axes[0]] = tangent_u
                coords[tangent_axes[1]] = tangent_v
                face_nodes[face_index, 3 * tangent_v + tangent_u] = (
                    9 * coords[2] + 3 * coords[1] + coords[0]
                )
                face_weight[3 * tangent_v + tangent_u] = (
                    line_weights[tangent_u] * line_weights[tangent_v]
                )
    perm_table = np.zeros((8, 9), np.int32)
    for orient in range(8):
        for tangent_v in range(3):
            for tangent_u in range(3):
                moved_u, moved_v = (tangent_v, tangent_u) if orient // 4 else (tangent_u, tangent_v)
                if orient % 2:
                    moved_u = 2 - moved_u
                if orient // 2 % 2:
                    moved_v = 2 - moved_v
                perm_table[orient, 3 * tangent_v + tangent_u] = 3 * moved_v + moved_u
    inverse_table = np.zeros((8,), np.int32)
    for orient in range(8):
        for candidate in range(8):
            if np.all(perm_table[candidate][perm_table[orient]] == np.arange(9)):
                inverse_table[orient] = candidate
    place_table = np.zeros((6, 27, 9), np.float32)
    orient_mats = np.zeros((8, 9, 9), np.float32)
    for face_index in range(6):
        for face_node in range(9):
            place_table[face_index, face_nodes[face_index, face_node], face_node] = 1.0
    for orient in range(8):
        for face_node in range(9):
            orient_mats[orient, face_node, perm_table[orient, face_node]] = 1.0
    return (face_weight, inverse_table, place_table, orient_mats)


def time_matrix(count_times):
    table = [0.0] * count_times
    for offset in range(1, count_times):
        parity = (-1.0) ** offset
        phase = math.pi * offset / count_times
        table[offset] = (
            0.3 * parity * math.cos(phase) / math.sin(phase) + 1.2 * parity / count_times
        )
    matrix = [
        [table[(col_index - row_index) % count_times] for col_index in range(count_times)]
        for row_index in range(count_times)
    ]
    return (np.array(table, np.float32), np.array(matrix, np.float32))


def slot_maps(element_ids, face_ids, count_elems):
    face_weight, inverse_table, place_table, orient_mats = build_tables()
    onehot = (jnp.arange(count_elems, dtype=jnp.int32)[:, None] == element_ids[None, :]).astype(
        jnp.float32
    )
    face_hot = (jnp.arange(6, dtype=jnp.int32)[:, None] == face_ids[None, :]).astype(jnp.float32)
    select = jnp.einsum("kmn,ks->mns", jnp.asarray(place_table), face_hot)
    return (onehot, select)


def restrict_trace(state, onehot, select):
    face_weight, inverse_table, place_table, orient_mats = build_tables()
    gathered = jnp.dot(state, onehot, precision=highest, preferred_element_type=jnp.float32)
    gathered = gathered.reshape(5, 27, onehot.shape[1])
    trace = jnp.einsum("mns,vms->vns", select, gathered, precision=highest)
    return trace * jnp.asarray(face_weight)[None, :, None]


def apply_received(trace, orients, jacobian, live):
    face_weight, inverse_table, place_table, orient_mats = build_tables()
    orient_hot = (jnp.arange(8, dtype=jnp.int32)[:, None] == orients[None, :]).astype(jnp.float32)
    mapping = jnp.einsum("onm,os->nms", jnp.asarray(orient_mats), orient_hot)
    permuted = jnp.einsum("nms,vms->vns", mapping, trace, precision=highest)
    received = jnp.einsum(
        "uvs,uns->vns", jacobian.reshape(5, 5, jacobian.shape[1]), permuted, precision=highest
    )
    return jnp.where(live[None, None, :], received, 0.0)


def scatter_back(received, select, onehot):
    placed = jnp.einsum("mns,vns->vms", select, received, precision=highest)
    placed = placed.reshape(5 * 27, onehot.shape[1])
    return jnp.dot(placed, onehot.T, precision=highest, preferred_element_type=jnp.float32)


def on_device(
    inverse,
    start,
    source,
    mass,
    inner_elem,
    inner_face,
    inner_orient,
    inner_jac,
    cross_elem,
    cross_face,
    cross_orient,
    cross_count,
    cross_jac,
):
    face_weight, inverse_table, place_table, orient_mats = build_tables()
    count_elems = start.shape[2]
    count_mesh = lax.axis_size("mesh")
    own_part = lax.axis_index("mesh")
    count_times = lax.axis_size("tm")
    own_time = lax.axis_index("tm")
    slot_cap = cross_elem.shape[1] // 5
    coef_table, coef_matrix = time_matrix(count_times)
    offsets = [1, count_mesh - 1, count_mesh // 2 - 1, count_mesh // 2, count_mesh // 2 + 1]
    back_orient = jnp.sum(
        jnp.where(
            inner_orient[None, :] == jnp.arange(8, dtype=jnp.int32)[:, None],
            jnp.asarray(inverse_table)[:, None],
            0,
        ),
        axis=0,
    ).astype(jnp.int32)
    inner_send_hot, inner_send_sel = slot_maps(
        jnp.concatenate([inner_elem[1], inner_elem[0]]),
        jnp.concatenate([inner_face[1], inner_face[0]]),
        count_elems,
    )
    inner_recv_hot, inner_recv_sel = slot_maps(
        jnp.concatenate([inner_elem[0], inner_elem[1]]),
        jnp.concatenate([inner_face[0], inner_face[1]]),
        count_elems,
    )
    inner_orients = jnp.concatenate([inner_orient, back_orient])
    inner_jacobian = jnp.concatenate([inner_jac[0, 0], inner_jac[0, 1]], axis=1)
    inner_live = jnp.ones((inner_orients.shape[0],), bool)
    own_elem = cross_elem[0].reshape(5, slot_cap)
    own_face = cross_face[0].reshape(5, slot_cap)
    mirror_index = np.array(mirror_list, np.int32)
    send_hot, send_sel = slot_maps(
        own_elem[mirror_index].reshape(-1), own_face[mirror_index].reshape(-1), count_elems
    )
    cross_hot, cross_sel = slot_maps(cross_elem[0], cross_face[0], count_elems)
    slot_pos = jnp.arange(5 * slot_cap, dtype=jnp.int32) % slot_cap
    cross_live = slot_pos < jnp.repeat(cross_count[0], slot_cap)
    cross_orients = cross_orient[0]
    cross_jacobian = cross_jac[0, :, 0, :]
    current = start[0]
    for sweep_index in range(SWEEPS):
        inner_trace = restrict_trace(current, inner_send_hot, inner_send_sel)
        inner_part = scatter_back(
            apply_received(inner_trace, inner_orients, inner_jacobian, inner_live),
            inner_recv_sel,
            inner_recv_hot,
        )
        piece = lax.all_gather(current[None], "tm", axis=0, tiled=True)
        instance_ids = jnp.arange(piece.shape[0], dtype=jnp.int32)
        offset_ids = (instance_ids - own_time) % count_times
        weights = jnp.sum(
            jnp.where(
                offset_ids[:, None] == jnp.arange(count_times, dtype=jnp.int32)[None, :],
                jnp.asarray(coef_table)[None, :],
                0.0,
            ),
            axis=1,
        )
        spectral = jnp.zeros_like(current) + jnp.einsum(
            "k,kie->ie", weights, piece, precision=highest
        )
        traces = restrict_trace(current, send_hot, send_sel).reshape(45, 5 * slot_cap)
        outgoing = jnp.zeros((45, count_mesh * slot_cap), jnp.float32)
        for place_index in range(5):
            target = (own_part - offsets[place_index]) % count_mesh * slot_cap
            outgoing = lax.dynamic_update_slice_in_dim(
                outgoing,
                traces[:, place_index * slot_cap : (place_index + 1) * slot_cap],
                target,
                1,
            )
        incoming = lax.all_to_all(outgoing, "mesh", split_axis=1, concat_axis=1, tiled=True)
        arrived_parts = []
        for place_index in range(5):
            anchor = (own_part + offsets[place_index]) % count_mesh * slot_cap
            arrived_parts.append(lax.dynamic_slice_in_dim(incoming, anchor, slot_cap, 1))
        arrived = jnp.concatenate(arrived_parts, axis=1).reshape(5, 9, 5 * slot_cap)
        cross_part = scatter_back(
            apply_received(arrived, cross_orients, cross_jacobian, cross_live), cross_sel, cross_hot
        )
        resid = (source[0] - inner_part - cross_part - mass * spectral).astype(jnp.bfloat16)
        current = jnp.einsum("ije,je->ie", inverse[0], resid, preferred_element_type=jnp.float32)
    return current[None]


def solution(mesh):
    in_specs = (
        P("tm", None, None, "mesh"),
        P("tm", None, "mesh"),
        P("tm", None, "mesh"),
        P(None, "mesh"),
        P(None, "mesh"),
        P(None, "mesh"),
        P("mesh"),
        P("tm", None, None, "mesh"),
        P("mesh", None),
        P("mesh", None),
        P("mesh", None),
        P("mesh", None),
        P("tm", None, "mesh", None),
    )
    out_specs = P("tm", None, "mesh")
    return jax.shard_map(
        on_device, mesh=mesh, in_specs=in_specs, out_specs=out_specs, check_vma=False
    )
```

profile of v0, /device:TPU:24, one launch (start us, length us, event | category | flops | bytes accessed | tf_op | source)
XLA Modules:
  0.0 354.4 jit_solution(5961202997579660574)
XLA Ops:
  14.9 2.7 reshape.162
  17.6 16.4 %all-to-all-start = ((f32[64,1,1440]{2,1,0:T(1,128)}), f32[64,1,1440]{2,1,0:T(1,128)}, u32[]{:S(2)}, u32[]{:S(2)}) async-start(f32[64,1,1440]{2,1,0:T(1,128)} %reshape.162), calls=%async_computation | async-start | bytes 786432 | tf_op jit(solution)/shard_map/all_to_all | solution.py:199
  34.5 3.7 %copy.118 = f32[27,9,512]{0,1,2:T(8,128)} copy(f32[27,9,512]{2,0,1:T(8,128)S(1)} %fusion.59) | data formatting | bytes 995328 | tf_op jit(solution)/shard_map/kmn,ks->mns/dot_general | solution.py:82
  39.4 3.7 %copy.116 = f32[9,9,512]{1,0,2:T(8,128)} copy(f32[9,9,512]{2,1,0:T(8,128)S(1)} %fusion.56) | data formatting | bytes 331776 | tf_op jit(solution)/shard_map/onm,os->nms/dot_general | solution.py:97
  46.9 3.7 %copy.115 = f32[27,9,512]{0,1,2:T(8,128)} copy(f32[27,9,512]{2,0,1:T(8,128)S(1)} %fusion.53) | data formatting | bytes 995328 | tf_op jit(solution)/shard_map/kmn,ks->mns/dot_general | solution.py:82
  50.6 9.1 %fusion.86 = f32[512,5,9]{2,1,0:T(8,128)S(1)} fusion(f32[5,27,512]{1,0,2:T(8,128)} %copy.114, f32[27,9,512]{0,1,2:T(8,128)} %copy.115), kind=kOutput, calls=%fused_computation.133 | convolution fusion | flops 7464960 | bytes 866304 | tf_op jit(solution)/shard_map/mns,vms->vns/dot_general | solution.py:90
  59.7 6.7 %fusion.12 = f32[512,5,9]{2,1,0:T(8,128)S(1)} fusion(f32[9,9,512]{1,0,2:T(8,128)S(1)} %copy-done.2, f32[512,5,9]{2,1,0:T(8,128)S(1)} %fusion.86, f32[9]{0:T(128)S(1)} %copy-done.27), kind=kOutput, calls=%fused_computation.16 | convolution fusion | flops 2511360 | bytes 350244 | tf_op jit(solution)/shard_map/nms,vms->vns/dot_general | solution.py:98
  66.5 3.6 %fusion.10 = f32[512,9,5]{1,2,0:T(8,128)S(1)} fusion(f32[5,5,512]{0,1,2:T(8,128)S(1)} %copy.117, f32[512,5,9]{2,1,0:T(8,128)S(1)} %fusion.12), kind=kOutput, calls=%fused_computation.14 | convolution fusion | flops 1382400 | bytes 235520 | tf_op jit(solution)/shard_map/uvs,uns->vns/dot_general | solution.py:99
  70.1 15.6 %fusion.16 = f32[5,27,512]{1,0,2:T(8,128)} fusion(f32[27,9,512]{0,1,2:T(8,128)S(1)} %copy-done, f32[512,9,5]{1,2,0:T(8,128)S(1)} %fusion.10), kind=kOutput, calls=%fused_computation.20 | convolution fusion | flops 7464960 | bytes 866304 | tf_op jit(solution)/shard_map/mns,vns->vms/dot_general | solution.py:106
  104.0 64.0 %all_gather.6 = f32[8,135,128]{2,1,0:T(8,128)S(1)} all-gather(f32[1,135,128]{2,1,0:T(8,128)S(1)} %copy-done.17), channel_id=1, replica_groups=mesh['tm'=8,'mesh'=64] {'tm'}, dimensions={0}, use_global_device_ids=true | all-gather | bytes 622080 | tf_op jit(solution)/shard_map/all_gather | solution.py:175
  169.7 3.3 reduce.17
  172.9 3.5 reshape.163
  180.9 3.4 convolution_bitcast_fusion.3
  191.0 3.9 %fusion = f32[128,135]{0,1:T(8,128)S(1)} fusion(f32[128,135]{0,1:T(8,128)S(1)} %fusion.33, bf16[1,135,135,128]{3,2,1,0:T(8,128)(2,1)} %param.30), kind=kLoop, calls=%fused_computation.4 | loop fusion | flops 6981120 | bytes 4803840 | tf_op jit(solution)/shard_map/ije,je->ie/dot_general | solution.py:209
  198.6 3.0 copy.131
  201.5 9.3 %fusion.87 = f32[512,5,9]{2,1,0:T(8,128)S(1)} fusion(f32[5,27,512]{1,0,2:T(8,128)} %copy.131, f32[27,9,512]{0,1,2:T(8,128)} %copy.115), kind=kOutput, calls=%fused_computation.134 | convolution fusion | flops 7464960 | bytes 866304 | tf_op jit(solution)/shard_map/mns,vms->vns/dot_general | solution.py:90
  210.8 8.1 %fusion.6 = f32[512,5,9]{2,1,0:T(8,128)} fusion(f32[9,9,512]{1,0,2:T(8,128)S(1)} %copy-done.3, f32[512,5,9]{2,1,0:T(8,128)S(1)} %fusion.87, f32[9]{0:T(128)S(1)} %copy-done.28), kind=kOutput, calls=%fused_computation.10 | convolution fusion | flops 2511360 | bytes 350244 | tf_op jit(solution)/shard_map/nms,vms->vns/dot_general | solution.py:98
  222.5 4.5 %fusion.23 = f32[5,9,160]{1,0,2:T(8,128)} fusion(f32[5,27,160]{1,0,2:T(8,128)} %copy.137, f32[27,9,160]{0,1,2:T(8,128)} %copy-done.6, f32[9]{0:T(128)S(1)} %copy-done.28), kind=kOutput, calls=%fused_computation.25 | convolution fusion | flops 2340000 | bytes 270756 | tf_op jit(solution)/shard_map/mns,vms->vns/dot_general | solution.py:90
  243.4 3.6 %reshape.164 = f32[64,1,1440]{2,1,0:T(1,128)} reshape(f32[64,32,45]{2,1,0:T(8,128)} %bitcast.168) | data formatting | bytes 737280
  247.0 15.4 %all-to-all-start.1 = ((f32[64,1,1440]{2,1,0:T(1,128)}), f32[64,1,1440]{2,1,0:T(1,128)}, u32[]{:S(2)}, u32[]{:S(2)}) async-start(f32[64,1,1440]{2,1,0:T(1,128)} %reshape.164), calls=%async_computation.1 | async-start | bytes 786432 | tf_op jit(solution)/shard_map/all_to_all | solution.py:199
  262.4 5.4 %fusion.4 = f32[512,9,5]{1,2,0:T(8,128)S(1)} fusion(f32[5,5,512]{0,1,2:T(8,128)S(1)} %copy.117, f32[512,5,9]{2,1,0:T(8,128)} %fusion.6), kind=kOutput, calls=%fused_computation.8 | convolution fusion | flops 1382400 | bytes 235520 | tf_op jit(solution)/shard_map/uvs,uns->vns/dot_general | solution.py:99
  267.8 3.7 %fusion.19 = f32[5,27,512]{1,0,2:T(8,128)S(1)} fusion(f32[27,9,512]{0,1,2:T(8,128)S(1)} %copy-done.1, f32[512,9,5]{1,2,0:T(8,128)S(1)} %fusion.4), kind=kOutput, calls=%fused_computation.21 | convolution fusion | flops 7464960 | bytes 866304 | tf_op jit(solution)/shard_map/mns,vns->vms/dot_general | solution.py:106
  274.7 64.1 %all-gather.1 = f32[8,135,128]{2,1,0:T(8,128)S(1)} all-gather(f32[1,135,128]{2,1,0:T(8,128)S(1)} %bitcast.171), channel_id=2, replica_groups=mesh['tm'=8,'mesh'=64] {'tm'}, dimensions={0}, use_global_device_ids=true | all-gather | bytes 622080 | tf_op jit(solution)/shard_map/all_gather | solution.py:175
  349.5 3.9 %fusion.1 = f32[128,135]{0,1:T(8,128)S(1)} fusion(f32[128,135]{0,1:T(8,128)S(1)} %fusion.31, bf16[1,135,135,128]{3,2,1,0:T(8,128)(2,1)} %param.30), kind=kLoop, calls=%fused_computation.5 | loop fusion | flops 6981120 | bytes 4803840 | tf_op jit(solution)/shard_map/ije,je->ie/dot_general | solution.py:209
  (195 shorter events, 89.2 us)
Async XLA Ops:
  0.0 9.0 %copy-start.27 = (f32[9]{0:T(128)S(1)}, f32[9]{0:T(128)}, u32[]{:S(2)}) copy-start(f32[9]{0:T(128)} %constant.153.clone) | copy-start | bytes 112
  11.8 22.3 %copy-start.34 = (s32[2,256]{1,0:T(2,128)S(1)}, s32[2,256]{1,0:T(2,128)}, u32[]{:S(2)}) copy-start(s32[2,256]{1,0:T(2,128)} %param.35) | copy-start | bytes 6148
  11.8 22.3 %copy-start.29 = (s32[256]{0:T(256)S(1)}, s32[256]{0:T(256)}, u32[]{:S(2)}) copy-start(s32[256]{0:T(256)} %param.36) | copy-start | bytes 3076
  11.8 22.3 %copy-start.37 = (s32[8]{0:T(128)S(1)}, s32[8]{0:T(128)}, u32[]{:S(2)}) copy-start(s32[8]{0:T(128)} %constant.149.clone) | copy-start | bytes 100
  11.8 22.4 %copy-start.10 = (bf16[6,27,9]{1,0,2:T(8,128)(2,1)S(1)}, bf16[6,27,9]{1,0,2:T(8,128)(2,1)}, u32[]{:S(2)}) copy-start(bf16[6,27,9]{1,0,2:T(8,128)(2,1)} %constant.251) | copy-start | bytes 8752
  17.6 151.6 %all-to-all-start = ((f32[64,1,1440]{2,1,0:T(1,128)}), f32[64,1,1440]{2,1,0:T(1,128)}, u32[]{:S(2)}, u32[]{:S(2)}) async-start(f32[64,1,1440]{2,1,0:T(1,128)} %reshape.162), calls=%async_computation | async-start | bytes 786432 | tf_op jit(solution)/shard_map/all_to_all | solution.py:199
  39.4 4.9 %copy-start.9 = (f32[1,135,128]{2,0,1:T(1,128)S(1)}, f32[1,135,128]{2,0,1:T(1,128)}, u32[]{:S(2)}) copy-start(f32[1,135,128]{2,0,1:T(1,128)} %param.31) | copy-start | bytes 207364
  50.6 9.2 %copy-start.2 = (f32[9,9,512]{1,0,2:T(8,128)S(1)}, f32[9,9,512]{1,0,2:T(8,128)}, u32[]{:S(2)}) copy-start(f32[9,9,512]{1,0,2:T(8,128)} %copy.116) | copy-start | bytes 497668
  70.1 15.6 %copy-start.36 = (s32[1,160]{1,0:T(1,128)S(1)}, s32[1,160]{1,0:T(1,128)}, u32[]{:S(2)}) copy-start(s32[1,160]{1,0:T(1,128)} %param.40) | copy-start | bytes 1924
  90.1 12.0 %copy-start.11 = (f32[1,135,128]{2,0,1:T(1,128)S(1)}, f32[1,135,128]{2,0,1:T(1,128)}, u32[]{:S(2)}) copy-start(f32[1,135,128]{2,0,1:T(1,128)} %param.32) | copy-start | bytes 207364
  90.1 12.0 %copy-start.20 = (s32[512]{0:T(512)S(1)}, s32[512]{0:T(512)}, u32[]{:S(2)}) copy-start(s32[512]{0:T(512)} %get-tuple-element.27) | copy-start | bytes 6148
  90.1 13.9 %copy-start.17 = (f32[1,135,128]{2,1,0:T(8,128)S(1)}, f32[1,135,128]{2,1,0:T(8,128)}, u32[]{:S(2)}) copy-start(f32[1,135,128]{2,1,0:T(8,128)} %copy.172) | copy-start | bytes 207364
  101.4 66.5 %copy-start.32 = (f32[8]{0:T(128)}, f32[8]{0:T(128)S(1)}, u32[]{:S(2)}) copy-start(f32[8]{0:T(128)S(1)} %select_reduce_fusion.1) | copy-start | bytes 100
  102.1 82.2 %copy-start.30 = (pred[160]{0:T(512)(128)(4,1)}, pred[160]{0:T(512)(128)(4,1)S(1)}, u32[]{:S(2)}) copy-start(pred[160]{0:T(512)(128)(4,1)S(1)} %fusion.76) | copy-start | bytes 484
  180.9 4.7 %copy-start.4 = (f32[27,9,160]{0,1,2:T(8,128)S(1)}, f32[27,9,160]{0,1,2:T(8,128)}, u32[]{:S(2)}) copy-start(f32[27,9,160]{0,1,2:T(8,128)} %copy.128) | copy-start | bytes 466564
  185.6 4.1 %copy-start.13 = (f32[1,135,128]{2,0,1:T(1,128)S(1)}, f32[1,135,128]{2,0,1:T(1,128)}, u32[]{:S(2)}) copy-start(f32[1,135,128]{2,0,1:T(1,128)} %fusion.38) | copy-start | bytes 207364
  185.6 4.1 %copy-start.14 = (f32[135,128]{1,0:T(8,128)S(1)}, f32[135,128]{1,0:T(8,128)}, u32[]{:S(2)}) copy-start(f32[135,128]{1,0:T(8,128)} %param.33) | copy-start | bytes 207364
  185.6 4.0 %copy-start.25 = (s32[1,160]{1,0:T(1,128)S(1)}, s32[1,160]{1,0:T(1,128)}, u32[]{:S(2)}) copy-start(s32[1,160]{1,0:T(1,128)} %param.38) | copy-start | bytes 1924
  191.0 5.0 %copy-start.24 = (s32[160]{0:T(256)S(1)}, s32[160]{0:T(256)}, u32[]{:S(2)}) copy-start(s32[160]{0:T(256)} %copy-done.23) | copy-start | bytes 1924
  201.5 9.3 %copy-start.3 = (f32[9,9,512]{1,0,2:T(8,128)S(1)}, f32[9,9,512]{1,0,2:T(8,128)}, u32[]{:S(2)}) copy-start(f32[9,9,512]{1,0,2:T(8,128)} %copy.116) | copy-start | bytes 497668
  201.5 9.3 %copy-start.28 = (f32[9]{0:T(128)S(1)}, f32[9]{0:T(128)}, u32[]{:S(2)}) copy-start(f32[9]{0:T(128)} %constant.153.clone) | copy-start | bytes 112
  247.0 92.4 %all-to-all-start.1 = ((f32[64,1,1440]{2,1,0:T(1,128)}), f32[64,1,1440]{2,1,0:T(1,128)}, u32[]{:S(2)}, u32[]{:S(2)}) async-start(f32[64,1,1440]{2,1,0:T(1,128)} %reshape.164), calls=%async_computation.1 | async-start | bytes 786432 | tf_op jit(solution)/shard_map/all_to_all | solution.py:199
  262.4 5.4 %copy-start.1 = (f32[27,9,512]{0,1,2:T(8,128)S(1)}, f32[27,9,512]{0,1,2:T(8,128)}, u32[]{:S(2)}) copy-start(f32[27,9,512]{0,1,2:T(8,128)} %copy.118) | copy-start | bytes 1492996
  271.5 67.3 %copy-start.33 = (f32[8]{0:T(128)S(1)}, f32[8]{0:T(128)}, u32[]{:S(2)}) copy-start(f32[8]{0:T(128)} %copy-done.32) | copy-start | bytes 100
  (16 other events, 40.7 us)
where the time goes:
time: 358 us; the launch traced here: 354 us
  blocking collectives  128 us (36%)
  matrix products  92.6 us (26%)
  local copies, waits for them, and re-layouts  80.1 us (22%)
  starting transfers between devices  31.8 us (9%)
  other arithmetic  20.7 us (6%)
    all_gather x2, blocking collectives, on_device(): piece = lax.all_gather(current[None], 'tm', axis=0, tiled=True)  128 us
    all_to_all x2, starting transfers between devices, on_device(): lax.all_to_all(outgoing, 'mesh', split_axis=1, concat_axis=1, tiled=True)  31.8 us
    dot_general x4, matrix products, restrict_trace(): trace = jnp.einsum('mns,vms->vns', select, gathered, precision=highest)  25.1 us
    dot_general x4, matrix products, scatter_back(): placed = jnp.einsum('mns,vns->vms', select, received, precision=highest)  22.6 us
    dot_general x4, matrix products, apply_received(): permuted = jnp.einsum('nms,vms->vns', mapping, trace, precision=highest)  20.4 us
    unnamed x102, local copies, waits for them, and re-layouts  18.6 us
    dot_general x4, matrix products, apply_received(): jnp.einsum('uvs,uns->vns', jacobian.reshape(5, 5, jacobian.shape[1]), per...  11.4 us
    reshape x8, local copies, waits for them, and re-layouts, restrict_trace(): gathered = gathered.reshape(5, 27, onehot.shape[1])  10.7 us
  transfers between devices with their start and end apart: 2, of which 0 were waited for; matrix products, arithmetic and copies ran while one was open for 23% of the time, Pallas kernels for 0%

commit v1 on v0

v1 whole, which is shorter than its diff:
```python
import functools
import math

import jax
import jax.numpy as jnp
import numpy as np
from jax import lax
from jax.experimental import pallas as pl
from jax.experimental.pallas import tpu as pltpu
from jax.sharding import PartitionSpec as P

SWEEPS = 2
LINE = (1.0 / 3.0, 4.0 / 3.0, 1.0 / 3.0)
CHUNKS = 9
VMEM = pl.BlockSpec(memory_space=pltpu.VMEM)
SMEM = pl.BlockSpec(memory_space=pltpu.SMEM)


def face_node(face, n):
    normal = face // 2
    tangent = [axis for axis in range(3) if axis != normal]
    coords = [0, 0, 0]
    coords[normal] = 2 * (face % 2)
    coords[tangent[0]] = n % 3
    coords[tangent[1]] = n // 3
    return 9 * coords[2] + 3 * coords[1] + coords[0]


NODE = [[face_node(face, n) for n in range(9)] for face in range(6)]
WEIGHT = [float(np.float32(LINE[n % 3] * LINE[n // 3])) for n in range(9)]


def coef_table(times):
    table = [0.0] * times
    for k in range(1, times):
        sign = (-1.0) ** k
        phase = math.pi * k / times
        table[k] = float(
            np.float32(0.3 * sign * math.cos(phase) / math.sin(phase) + 1.2 * sign / times)
        )
    return table


def split_rows(value):
    high = value.astype(jnp.bfloat16).astype(jnp.float32)
    return jnp.concatenate([high, value - high], axis=0).astype(jnp.bfloat16)


def join_rows(value):
    half = value.shape[0] // 2
    return value[:half] + value[half:]


def face_rows(x_ref):
    elems = x_ref.shape[1]
    pad = jnp.zeros((3, elems), jnp.float32)
    nodes = [
        jnp.concatenate([x_ref[pl.ds(m, 5, stride=27), :], pad], axis=0) for m in range(27)
    ]
    blocks = []
    for face in range(6):
        rows = jnp.concatenate([nodes[NODE[face][n]] * WEIGHT[n] for n in range(9)], axis=0)
        blocks.append(split_rows(rows))
    return jnp.concatenate(blocks, axis=1)


def onehot(code, elems):
    slots = code.shape[1]
    row = lax.broadcasted_iota(jnp.int32, (elems, slots), 0)
    parts = [
        jnp.where(row == code - face * elems, 1.0, 0.0).astype(jnp.bfloat16) for face in range(6)
    ]
    return jnp.concatenate(parts, axis=0)


def cross_code(elem_ref, face_ref, elems, order):
    code = face_ref[...] * elems + elem_ref[...]
    cap = code.shape[1] // 5
    parts = [code[:, k * cap : (k + 1) * cap] for k in order]
    fill = 256 - code.shape[1]
    return jnp.concatenate(parts + [jnp.full((1, fill), -1, jnp.int32)], axis=1)


def cross_trace(x_ref, elem_ref, face_ref, near_ref, far_ref):
    hot = onehot(cross_code(elem_ref, face_ref, x_ref.shape[1], (0, 4, 1, 2, 3)), x_ref.shape[1])
    trace = join_rows(jnp.dot(face_rows(x_ref), hot, preferred_element_type=jnp.float32))
    near_ref[...] = trace[:, :128]
    far_ref[...] = trace[:, 128:]


def received_rows(trace, orient, jacobian):
    slots = trace.shape[1]
    code = jnp.broadcast_to(orient, (8, slots))
    flip_i = (code & 1) == 1
    flip_j = ((code >> 1) & 1) == 1
    swap = code >= 4
    tile = [trace[8 * n : 8 * n + 8] for n in range(9)]
    for j in range(3):
        low, high = tile[3 * j], tile[3 * j + 2]
        tile[3 * j] = jnp.where(flip_i, high, low)
        tile[3 * j + 2] = jnp.where(flip_i, low, high)
    for i in range(3):
        low, high = tile[i], tile[6 + i]
        tile[i] = jnp.where(flip_j, high, low)
        tile[6 + i] = jnp.where(flip_j, low, high)
    for j in range(3):
        for i in range(j):
            one, two = tile[3 * j + i], tile[3 * i + j]
            tile[3 * j + i] = jnp.where(swap, two, one)
            tile[3 * i + j] = jnp.where(swap, one, two)
    rows = []
    for n in range(9):
        total = jacobian[0] * tile[n][0:1]
        for u in range(1, 5):
            total = total + jacobian[u] * tile[n][u : u + 1]
        rows.append(total)
    return jnp.concatenate(rows, axis=0)


def scatter_nodes(rows, hot, elems):
    placed = join_rows(
        lax.dot_general(
            split_rows(rows), hot, (((1,), (1,)), ((), ())), preferred_element_type=jnp.float32
        )
    )
    nodes = [None] * 27
    for face in range(6):
        for n in range(9):
            part = placed[8 * n : 8 * n + 8, face * elems : (face + 1) * elems]
            m = NODE[face][n]
            nodes[m] = part if nodes[m] is None else nodes[m] + part
    return nodes


def inner_kernel(x_ref, elem_ref, face_ref, orient_ref, jac_ref, out_ref):
    elems = x_ref.shape[1]
    half = elem_ref.shape[1]
    code = face_ref[...] * elems + elem_ref[...]
    hot = onehot(jnp.concatenate([code[0:1], code[1:2]], axis=1), elems)
    trace = join_rows(jnp.dot(face_rows(x_ref), hot, preferred_element_type=jnp.float32))
    trace = jnp.concatenate([trace[:, half:], trace[:, :half]], axis=1)
    orient = orient_ref[...]
    back = jnp.where(orient >= 4, 4 + 2 * (orient & 1) + ((orient >> 1) & 1), orient)
    pad = jnp.zeros((3, 2 * half), jnp.float32)
    jacobian = []
    for u in range(5):
        rows = jnp.concatenate(
            [jac_ref[0, side, 5 * u : 5 * u + 5, :] for side in range(2)], axis=1
        )
        jacobian.append(jnp.concatenate([rows, pad], axis=0))
    rows = received_rows(trace, jnp.concatenate([orient, back], axis=1), jacobian)
    nodes = scatter_nodes(rows, hot, elems)
    for m in range(27):
        out_ref[8 * m : 8 * m + 8, :] = (
            nodes[m] if nodes[m] is not None else jnp.zeros((8, elems), jnp.float32)
        )


def combine_kernel(times, x_ref, z_ref, one_ref, two_ref, three_ref):
    table = coef_table(times)
    half = times // 2
    y = lax.axis_index("tm") % half
    x = x_ref[...]
    z = z_ref[...]
    for step, out in ((1, one_ref), (2, two_ref), (3, three_ref)):
        wraps = y + step >= half
        first = table[times - step]
        second = table[half - step]
        out[...] = x * jnp.where(wraps, second, first) + z * jnp.where(wraps, first, second)


def relay_kernel(cap, even_ref, odd_ref, far_ref, out_ref):
    is_even = lax.axis_index("mesh") % 2 == 0
    even = even_ref[...]
    odd = odd_ref[...]
    above = jnp.where(is_even, even, odd)
    below = jnp.where(is_even, odd, even)
    out_ref[...] = jnp.concatenate(
        [far_ref[:, :cap], below[:, cap : 2 * cap], above[:, 3 * cap : 4 * cap], far_ref[:, :cap]],
        axis=1,
    )


def final_kernel(
    cap,
    last,
    table_half,
    inner_ref,
    even_ref,
    odd_ref,
    far_ref,
    elem_ref,
    face_ref,
    orient_ref,
    count_ref,
    jac_ref,
    source_ref,
    mass_ref,
    z_ref,
    one_ref,
    two_ref,
    three_ref,
    inverse_ref,
    *rest,
):
    if last:
        out_ref, resid_ref, held_ref, sems = rest
    else:
        out_ref, near_ref, send_ref, resid_ref, held_ref, sems = rest
    size, elems = source_ref.shape
    per = size // CHUNKS
    copies = []
    for c in range(CHUNKS):
        copy = pltpu.make_async_copy(
            inverse_ref.at[0, pl.ds(c * per, per)], held_ref.at[pl.ds(c * per, per)], sems.at[c]
        )
        copy.start()
        copies.append(copy)

    is_even = lax.axis_index("mesh") % 2 == 0
    even = even_ref[...]
    odd = odd_ref[...]
    far = far_ref[...]
    above = jnp.where(is_even, even, odd)
    below = jnp.where(is_even, odd, even)
    slots = 5 * cap
    fill = 256 - slots
    trace = jnp.concatenate(
        [
            above[:, 2 * cap : 3 * cap],
            below[:, :cap],
            far[:, cap : 2 * cap],
            far[:, :cap],
            far[:, 2 * cap : 3 * cap],
            jnp.zeros((72, fill), jnp.float32),
        ],
        axis=1,
    )
    hot = onehot(cross_code(elem_ref, face_ref, elems, range(5)), elems)
    orient = jnp.concatenate([orient_ref[...], jnp.zeros((1, fill), jnp.int32)], axis=1)
    lane = lax.broadcasted_iota(jnp.int32, (8, 256), 1)
    live = lane < 0
    for k in range(5):
        live = live | ((lane >= k * cap) & (lane < k * cap + count_ref[0, k]))
    jacobian = []
    for u in range(5):
        rows = jnp.concatenate(
            [jac_ref[5 * u : 5 * u + 5, :], jnp.zeros((5, fill), jnp.float32)], axis=1
        )
        rows = jnp.concatenate([rows, jnp.zeros((3, 256), jnp.float32)], axis=0)
        jacobian.append(jnp.where(live, rows, 0.0))
    nodes = scatter_nodes(received_rows(trace, orient, jacobian), hot, elems)
    for m in range(27):
        part = inner_ref[8 * m : 8 * m + 8, :]
        part = part if nodes[m] is None else part + nodes[m]
        resid_ref[pl.ds(m, 5, stride=27), :] = part[:5]
    spectral = z_ref[...] * table_half + one_ref[...] + two_ref[...] + three_ref[...]
    resid = source_ref[...] - resid_ref[...] - mass_ref[...] * spectral
    resid = resid.astype(jnp.bfloat16).astype(jnp.float32)
    for c in range(CHUNKS):
        copies[c].wait()

        def body(step, carry):
            for r in range(5):
                i = c * per + step * 5 + r
                product = held_ref[i].astype(jnp.float32) * resid
                out_ref[pl.ds(i, 1), :] = jnp.sum(product, axis=0, keepdims=True)
            return carry

        lax.fori_loop(0, per // 5, body, 0)
    if not last:
        cross_trace(out_ref, elem_ref, face_ref, near_ref, send_ref)


def on_device(
    inverse,
    start,
    source,
    mass,
    inner_elem,
    inner_face,
    inner_orient,
    inner_jac,
    cross_elem,
    cross_face,
    cross_orient,
    cross_count,
    cross_jac,
):
    size, elems = start.shape[1:]
    count_mesh = lax.axis_size("mesh")
    times = lax.axis_size("tm")
    half_times = times // 2
    cap = cross_elem.shape[1] // 5
    table = coef_table(times)
    f32 = jnp.float32
    state = jax.ShapeDtypeStruct((size, elems), f32)
    near_shape = jax.ShapeDtypeStruct((72, 128), f32)
    params = pltpu.CompilerParams(vmem_limit_bytes=40 * 1024 * 1024)

    across = [(t, (t + half_times) % times) for t in range(times)]
    around = [
        [(t, t // half_times * half_times + (t + step) % half_times) for t in range(times)]
        for step in (1, 2, 3)
    ]
    evens = [(p, p ^ 1) for p in range(count_mesh)]
    odds = [(p, ((p + 1) ^ 1) - 1) for p in range(count_mesh)]
    odds = [(p, q % count_mesh) for p, q in odds]
    opposite = [(p, (p + count_mesh // 2) % count_mesh) for p in range(count_mesh)]

    x = start[0]
    source = source[0]
    orient_row = inner_orient[None, :]
    jac_row = cross_jac[0, :, 0, :]
    near, far = pl.pallas_call(
        cross_trace,
        out_shape=(near_shape, near_shape),
        in_specs=[VMEM] * 3,
        out_specs=(VMEM, VMEM),
        compiler_params=params,
    )(x, cross_elem, cross_face)
    for sweep in range(SWEEPS):
        last = sweep == SWEEPS - 1
        over = lax.ppermute(x, "tm", across)
        even = lax.ppermute(near, "mesh", evens)
        odd = lax.ppermute(near, "mesh", odds)
        inner = pl.pallas_call(
            inner_kernel,
            out_shape=jax.ShapeDtypeStruct((216, elems), f32),
            in_specs=[VMEM] * 5,
            out_specs=VMEM,
            compiler_params=params,
        )(x, inner_elem, inner_face, orient_row, inner_jac)
        parts = pl.pallas_call(
            functools.partial(combine_kernel, times),
            out_shape=(state,) * 3,
            in_specs=[VMEM] * 2,
            out_specs=(VMEM,) * 3,
            compiler_params=params,
        )(x, over)
        parts = [lax.ppermute(part, "tm", pairs) for part, pairs in zip(parts, around)]
        passed = pl.pallas_call(
            functools.partial(relay_kernel, cap),
            out_shape=near_shape,
            in_specs=[VMEM] * 3,
            out_specs=VMEM,
            compiler_params=params,
        )(even, odd, far)
        passed = lax.ppermute(passed, "mesh", opposite)
        result = pl.pallas_call(
            functools.partial(final_kernel, cap, last, table[half_times]),
            out_shape=(state,) if last else (state, near_shape, near_shape),
            in_specs=[VMEM] * 7 + [SMEM] + [VMEM] * 7 + [pl.BlockSpec(memory_space=pl.ANY)],
            out_specs=(VMEM,) if last else (VMEM,) * 3,
            scratch_shapes=[
                pltpu.VMEM((size, elems), f32),
                pltpu.VMEM((size, size, elems), jnp.bfloat16),
                pltpu.SemaphoreType.DMA((CHUNKS,)),
            ],
            compiler_params=params,
        )(
            inner,
            even,
            odd,
            passed,
            cross_elem,
            cross_face,
            cross_orient,
            cross_count,
            jac_row,
            source,
            mass,
            over,
            *parts,
            inverse,
        )
        if last:
            return result[0][None]
        x, near, far = result


def solution(mesh):
    in_specs = (
        P("tm", None, None, "mesh"),
        P("tm", None, "mesh"),
        P("tm", None, "mesh"),
        P(None, "mesh"),
        P(None, "mesh"),
        P(None, "mesh"),
        P("mesh"),
        P("tm", None, None, "mesh"),
        P("mesh", None),
        P("mesh", None),
        P("mesh", None),
        P("mesh", None),
        P("tm", None, "mesh", None),
    )
    out_specs = P("tm", None, "mesh")
    return jax.shard_map(
        on_device, mesh=mesh, in_specs=in_specs, out_specs=out_specs, check_vma=False
    )
```

time: 358 us -> 101 us (0.28)
  the two profiles are of different devices: /device:TPU:24 before, /device:TPU:16 now
where the time goes in v1:
time: 101 us; the launch traced here: 100 us
  starting transfers between devices  65.5 us (65%)
  Pallas kernels  13.7 us (14%)
  local copies, waits for them, and re-layouts  12 us (12%)
  waiting for transfers between devices  8.83 us (9%)
    ppermute x2, starting transfers between devices, on_device(): over = lax.ppermute(x, 'tm', across)  22.5 us
    ppermute x6, starting transfers between devices, on_device(): lax.ppermute(part, 'tm', pairs)  20.6 us
    pallas_call x2, Pallas kernels, on_device(): pl.pallas_call(functools.partial(final_kernel, cap, last, table[half_time...  11.5 us
    unnamed x28, local copies, waits for them, and re-layouts  11.3 us
    ppermute x2, starting transfers between devices, on_device(): odd = lax.ppermute(near, 'mesh', odds)  10.4 us
    ppermute x2, starting transfers between devices, on_device(): passed = lax.ppermute(passed, 'mesh', opposite)  7.85 us
    ppermute x2, waiting for transfers between devices, on_device(): passed = lax.ppermute(passed, 'mesh', opposite)  5.55 us
    ppermute x2, starting transfers between devices, on_device(): even = lax.ppermute(near, 'mesh', evens)  4.15 us
  transfers between devices with their start and end apart: 14, of which 3 were waited for; matrix products, arithmetic and copies ran while one was open for 2% of the time, Pallas kernels for 2%

profile of v1, /device:TPU:16, one launch (start us, length us, event | category | flops | bytes accessed | tf_op | source)
XLA Modules:
  0.0 100.3 jit_solution(5660381884746436014)
XLA Ops:
  0.0 0.9 copy.24
  0.9 15.7 %collective-permute-start.3 = (f32[135,128]{1,0:T(8,128)S(1)}, f32[135,128]{1,0:T(8,128)S(1)}, u32[]{:S(2)}, u32[]{:S(2)}) collective-permute-start(f32[135,128]{1,0:T(8,128)S(1)} %bitcast.11), channel_id=1, source_target_pairs={{0,256},{64,320},{128,384},{192,448},{256,0},{320,64},{384,128},{4... | collective-permute-start | bytes 207368 | tf_op jit(solution)/shard_map/ppermute | solution.py:324
  18.3 7.0 %collective-permute-start.1 = (f32[72,128]{1,0:T(8,128)S(1)}, f32[72,128]{1,0:T(8,128)S(1)}, u32[]{:S(2)}, u32[]{:S(2)}) collective-permute-start(f32[72,128]{1,0:T(8,128)S(1)} %get-tuple-element.16), channel_id=1, source_target_pairs={{0,63},{1,2},{2,1},{3,4},{4,3},{5,6},{6,5},{7,8},{8,7},{9,10},{10,... | collective-permute-start | bytes 110600 | tf_op jit(solution)/shard_map/ppermute | solution.py:326
  25.4 1.9 %collective-permute-start = (f32[72,128]{1,0:T(8,128)S(1)}, f32[72,128]{1,0:T(8,128)S(1)}, u32[]{:S(2)}, u32[]{:S(2)}) collective-permute-start(f32[72,128]{1,0:T(8,128)S(1)} %get-tuple-element.16), channel_id=1, source_target_pairs={{0,1},{1,0},{2,3},{3,2},{4,5},{5,4},{6,7},{7,6},{8,9},{9,8},{10,11... | collective-permute-start | bytes 110600 | tf_op jit(solution)/shard_map/ppermute | solution.py:325
  27.3 3.2 %collective-permute-start.4 = (f32[135,128]{1,0:T(8,128)S(1)}, f32[135,128]{1,0:T(8,128)S(1)}, u32[]{:S(2)}, u32[]{:S(2)}) collective-permute-start(f32[135,128]{1,0:T(8,128)S(1)} %get-tuple-element.18), channel_id=1, source_target_pairs={{0,64},{64,128},{128,192},{192,0},{256,320},{320,384},{384,448},{4... | collective-permute-start | bytes 207368 | tf_op jit(solution)/shard_map/ppermute | solution.py:341
  30.5 2.5 %collective-permute-start.5 = (f32[135,128]{1,0:T(8,128)S(1)}, f32[135,128]{1,0:T(8,128)S(1)}, u32[]{:S(2)}, u32[]{:S(2)}) collective-permute-start(f32[135,128]{1,0:T(8,128)S(1)} %get-tuple-element.19), channel_id=1, source_target_pairs={{0,128},{64,192},{128,0},{192,64},{256,384},{320,448},{384,256},{4... | collective-permute-start | bytes 207368 | tf_op jit(solution)/shard_map/ppermute | solution.py:341
  33.1 3.0 %collective-permute-start.6 = (f32[135,128]{1,0:T(8,128)S(1)}, f32[135,128]{1,0:T(8,128)S(1)}, u32[]{:S(2)}, u32[]{:S(2)}) collective-permute-start(f32[135,128]{1,0:T(8,128)S(1)} %get-tuple-element.20), channel_id=1, source_target_pairs={{0,192},{64,0},{128,64},{192,128},{256,448},{320,256},{384,320},{4... | collective-permute-start | bytes 207368 | tf_op jit(solution)/shard_map/ppermute | solution.py:341
  36.2 2.8 %collective-permute-start.2 = (f32[72,128]{1,0:T(8,128)S(1)}, f32[72,128]{1,0:T(8,128)S(1)}, u32[]{:S(2)}, u32[]{:S(2)}) collective-permute-start(f32[72,128]{1,0:T(8,128)S(1)} %shard_map.129), channel_id=1, source_target_pairs={{0,32},{1,33},{2,34},{3,35},{4,36},{5,37},{6,38},{7,39},{8,40},{9,... | collective-permute-start | bytes 110600 | tf_op jit(solution)/shard_map/ppermute | solution.py:349
  39.7 0.8 copy.14.jac_ref
  40.5 0.9 copy.23
  44.2 1.7 %collective-permute-done.2.far_ref = f32[72,128]{1,0:T(8,128)S(1)} collective-permute-done((f32[72,128]{1,0:T(8,128)S(1)}, f32[72,128]{1,0:T(8,128)S(1)}, u32[]{:S(2)}, u32[]{:S(2)}) %collective-permute-start.2) | collective-permute-done | bytes 36896 | tf_op jit(solution)/shard_map/ppermute | solution.py:349
  46.0 2.3 %copy-done = bf16[1,135,135,128]{3,2,1,0:T(8,128)(2,1)S(1)} copy-done((bf16[1,135,135,128]{3,2,1,0:T(8,128)(2,1)S(1)}, bf16[1,135,135,128]{3,2,1,0:T(8,128)(2,1)}, u32[]{:S(2)}) %copy-start) | copy-done | bytes 4665624
  48.3 0.9 copy-done.2
  50.5 5.9 %shard_map.131 = (f32[135,128]{1,0:T(8,128)S(1)}, f32[72,128]{1,0:T(8,128)S(1)}, f32[72,128]{1,0:T(8,128)S(1)}) custom-call(f32[216,128]{1,0:T(8,128)S(1)} %shard_map.127.inner_ref, f32[72,128]{1,0:T(8,128)S(1)} %collective-permute-done.even_ref, f32[72,128]{1,0:T(8,128)S(1)} %collective-permute-done.1.odd_ref, ...), custom_call_target="tpu_custom_call" | custom-call | tf_op jit(solution)/shard_map/pallas_call | solution.py:350
  56.4 6.8 %collective-permute-start.10 = (f32[135,128]{1,0:T(8,128)S(1)}, f32[135,128]{1,0:T(8,128)S(1)}, u32[]{:S(2)}, u32[]{:S(2)}) collective-permute-start(f32[135,128]{1,0:T(8,128)S(1)} %get-tuple-element.21.x_ref), channel_id=1, source_target_pairs={{0,256},{64,320},{128,384},{192,448},{256,0},{320,64},{384,128},{4... | collective-permute-start | bytes 207368 | tf_op jit(solution)/shard_map/ppermute | solution.py:324
  63.2 3.4 %collective-permute-start.8 = (f32[72,128]{1,0:T(8,128)S(1)}, f32[72,128]{1,0:T(8,128)S(1)}, u32[]{:S(2)}, u32[]{:S(2)}) collective-permute-start(f32[72,128]{1,0:T(8,128)S(1)} %get-tuple-element.22), channel_id=1, source_target_pairs={{0,63},{1,2},{2,1},{3,4},{4,3},{5,6},{6,5},{7,8},{8,7},{9,10},{10,... | collective-permute-start | bytes 110600 | tf_op jit(solution)/shard_map/ppermute | solution.py:326
  66.6 2.2 %collective-permute-start.7 = (f32[72,128]{1,0:T(8,128)S(1)}, f32[72,128]{1,0:T(8,128)S(1)}, u32[]{:S(2)}, u32[]{:S(2)}) collective-permute-start(f32[72,128]{1,0:T(8,128)S(1)} %get-tuple-element.22), channel_id=1, source_target_pairs={{0,1},{1,0},{2,3},{3,2},{4,5},{5,4},{6,7},{7,6},{8,9},{9,8},{10,11... | collective-permute-start | bytes 110600 | tf_op jit(solution)/shard_map/ppermute | solution.py:325
  68.9 3.3 %collective-permute-done.10.z_ref = f32[135,128]{1,0:T(8,128)S(1)} collective-permute-done((f32[135,128]{1,0:T(8,128)S(1)}, f32[135,128]{1,0:T(8,128)S(1)}, u32[]{:S(2)}, u32[]{:S(2)}) %collective-permute-start.10) | collective-permute-done | bytes 69152 | tf_op jit(solution)/shard_map/ppermute | solution.py:324
  72.1 3.4 %collective-permute-start.11 = (f32[135,128]{1,0:T(8,128)S(1)}, f32[135,128]{1,0:T(8,128)S(1)}, u32[]{:S(2)}, u32[]{:S(2)}) collective-permute-start(f32[135,128]{1,0:T(8,128)S(1)} %get-tuple-element.24), channel_id=1, source_target_pairs={{0,64},{64,128},{128,192},{192,0},{256,320},{320,384},{384,448},{4... | collective-permute-start | bytes 207368 | tf_op jit(solution)/shard_map/ppermute | solution.py:341
  75.6 4.7 %collective-permute-start.12 = (f32[135,128]{1,0:T(8,128)S(1)}, f32[135,128]{1,0:T(8,128)S(1)}, u32[]{:S(2)}, u32[]{:S(2)}) collective-permute-start(f32[135,128]{1,0:T(8,128)S(1)} %get-tuple-element.25), channel_id=1, source_target_pairs={{0,128},{64,192},{128,0},{192,64},{256,384},{320,448},{384,256},{4... | collective-permute-start | bytes 207368 | tf_op jit(solution)/shard_map/ppermute | solution.py:341
  80.2 3.9 %collective-permute-start.13 = (f32[135,128]{1,0:T(8,128)S(1)}, f32[135,128]{1,0:T(8,128)S(1)}, u32[]{:S(2)}, u32[]{:S(2)}) collective-permute-start(f32[135,128]{1,0:T(8,128)S(1)} %get-tuple-element.26), channel_id=1, source_target_pairs={{0,192},{64,0},{128,64},{192,128},{256,448},{320,256},{384,320},{4... | collective-permute-start | bytes 207368 | tf_op jit(solution)/shard_map/ppermute | solution.py:341
  84.2 5.1 %collective-permute-start.9 = (f32[72,128]{1,0:T(8,128)S(1)}, f32[72,128]{1,0:T(8,128)S(1)}, u32[]{:S(2)}, u32[]{:S(2)}) collective-permute-start(f32[72,128]{1,0:T(8,128)S(1)} %shard_map.133), channel_id=1, source_target_pairs={{0,32},{1,33},{2,34},{3,35},{4,36},{5,37},{6,38},{7,39},{8,40},{9,... | collective-permute-start | bytes 110600 | tf_op jit(solution)/shard_map/ppermute | solution.py:349
  90.1 3.8 %collective-permute-done.9.far_ref = f32[72,128]{1,0:T(8,128)S(1)} collective-permute-done((f32[72,128]{1,0:T(8,128)S(1)}, f32[72,128]{1,0:T(8,128)S(1)}, u32[]{:S(2)}, u32[]{:S(2)}) %collective-permute-start.9) | collective-permute-done | bytes 36896 | tf_op jit(solution)/shard_map/ppermute | solution.py:349
  94.0 5.6 %shard_map.135 = f32[135,128]{1,0:T(8,128)S(1)} custom-call(f32[216,128]{1,0:T(8,128)S(1)} %shard_map.132.inner_ref, f32[72,128]{1,0:T(8,128)S(1)} %collective-permute-done.7.even_ref, f32[72,128]{1,0:T(8,128)S(1)} %collective-permute-done.8.odd_ref, f32[72,128]{1,0:T(8,128)S(1)} %collective-permute-done.9.far_ref, s32[1,160]{1,0:T(1,128)S(1)} %copy-done.4, ...), custom_call_target="tpu_custom_call" | custom-call | tf_op jit(solution)/shard_map/pallas_call | solution.py:350
  (42 shorter events, 8.4 us)
Async XLA Ops:
  0.0 89.3 %copy-start.7 = (s32[2,256]{1,0:T(2,128)S(1)}, s32[2,256]{1,0:T(2,128)}, u32[]{:S(2)}) copy-start(s32[2,256]{1,0:T(2,128)} %elem_ref.8) | copy-start | bytes 6148
  0.0 94.0 %copy-start.3 = (f32[135,128]{1,0:T(8,128)S(1)}, f32[135,128]{1,0:T(8,128)}, u32[]{:S(2)}) copy-start(f32[135,128]{1,0:T(8,128)} %mass_ref.3) | copy-start | bytes 207364
  0.9 26.4 %collective-permute-start.3 = (f32[135,128]{1,0:T(8,128)S(1)}, f32[135,128]{1,0:T(8,128)S(1)}, u32[]{:S(2)}, u32[]{:S(2)}) collective-permute-start(f32[135,128]{1,0:T(8,128)S(1)} %bitcast.11), channel_id=1, source_target_pairs={{0,256},{64,320},{128,384},{192,448},{256,0},{320,64},{384,128},{4... | collective-permute-start | bytes 207368 | tf_op jit(solution)/shard_map/ppermute | solution.py:324
  16.6 0.7 copy-start.4
  17.3 0.7 copy-start.5
  18.3 17.7 %collective-permute-start.1 = (f32[72,128]{1,0:T(8,128)S(1)}, f32[72,128]{1,0:T(8,128)S(1)}, u32[]{:S(2)}, u32[]{:S(2)}) collective-permute-start(f32[72,128]{1,0:T(8,128)S(1)} %get-tuple-element.16), channel_id=1, source_target_pairs={{0,63},{1,2},{2,1},{3,4},{4,3},{5,6},{6,5},{7,8},{8,7},{9,10},{10,... | collective-permute-start | bytes 110600 | tf_op jit(solution)/shard_map/ppermute | solution.py:326
  25.4 10.7 %collective-permute-start = (f32[72,128]{1,0:T(8,128)S(1)}, f32[72,128]{1,0:T(8,128)S(1)}, u32[]{:S(2)}, u32[]{:S(2)}) collective-permute-start(f32[72,128]{1,0:T(8,128)S(1)} %get-tuple-element.16), channel_id=1, source_target_pairs={{0,1},{1,0},{2,3},{3,2},{4,5},{5,4},{6,7},{7,6},{8,9},{9,8},{10,11... | collective-permute-start | bytes 110600 | tf_op jit(solution)/shard_map/ppermute | solution.py:325
  27.3 18.6 %collective-permute-start.4 = (f32[135,128]{1,0:T(8,128)S(1)}, f32[135,128]{1,0:T(8,128)S(1)}, u32[]{:S(2)}, u32[]{:S(2)}) collective-permute-start(f32[135,128]{1,0:T(8,128)S(1)} %get-tuple-element.18), channel_id=1, source_target_pairs={{0,64},{64,128},{128,192},{192,0},{256,320},{320,384},{384,448},{4... | collective-permute-start | bytes 207368 | tf_op jit(solution)/shard_map/ppermute | solution.py:341
  30.5 15.4 %collective-permute-start.5 = (f32[135,128]{1,0:T(8,128)S(1)}, f32[135,128]{1,0:T(8,128)S(1)}, u32[]{:S(2)}, u32[]{:S(2)}) collective-permute-start(f32[135,128]{1,0:T(8,128)S(1)} %get-tuple-element.19), channel_id=1, source_target_pairs={{0,128},{64,192},{128,0},{192,64},{256,384},{320,448},{384,256},{4... | collective-permute-start | bytes 207368 | tf_op jit(solution)/shard_map/ppermute | solution.py:341
  33.1 12.9 %collective-permute-start.6 = (f32[135,128]{1,0:T(8,128)S(1)}, f32[135,128]{1,0:T(8,128)S(1)}, u32[]{:S(2)}, u32[]{:S(2)}) collective-permute-start(f32[135,128]{1,0:T(8,128)S(1)} %get-tuple-element.20), channel_id=1, source_target_pairs={{0,192},{64,0},{128,64},{192,128},{256,448},{320,256},{384,320},{4... | collective-permute-start | bytes 207368 | tf_op jit(solution)/shard_map/ppermute | solution.py:341
  36.2 9.8 %collective-permute-start.2 = (f32[72,128]{1,0:T(8,128)S(1)}, f32[72,128]{1,0:T(8,128)S(1)}, u32[]{:S(2)}, u32[]{:S(2)}) collective-permute-start(f32[72,128]{1,0:T(8,128)S(1)} %shard_map.129), channel_id=1, source_target_pairs={{0,32},{1,33},{2,34},{3,35},{4,36},{5,37},{6,38},{7,39},{8,40},{9,... | collective-permute-start | bytes 110600 | tf_op jit(solution)/shard_map/ppermute | solution.py:349
  41.4 0.7 copy-start.6
  42.1 0.7 copy-start.8
  42.8 0.7 copy-start.9
  45.9 2.3 %copy-start = (bf16[1,135,135,128]{3,2,1,0:T(8,128)(2,1)S(1)}, bf16[1,135,135,128]{3,2,1,0:T(8,128)(2,1)}, u32[]{:S(2)}) copy-start(bf16[1,135,135,128]{3,2,1,0:T(8,128)(2,1)} %inverse_ref.3) | copy-start | bytes 13996804
  48.3 0.9 copy-start.2
  50.5 43.5 %copy-start.1 = (bf16[1,135,135,128]{3,2,1,0:T(8,128)(2,1)S(1)}, bf16[1,135,135,128]{3,2,1,0:T(8,128)(2,1)}, u32[]{:S(2)}) copy-start(bf16[1,135,135,128]{3,2,1,0:T(8,128)(2,1)} %inverse_ref.3) | copy-start | bytes 13996804
  56.4 15.7 %collective-permute-start.10 = (f32[135,128]{1,0:T(8,128)S(1)}, f32[135,128]{1,0:T(8,128)S(1)}, u32[]{:S(2)}, u32[]{:S(2)}) collective-permute-start(f32[135,128]{1,0:T(8,128)S(1)} %get-tuple-element.21.x_ref), channel_id=1, source_target_pairs={{0,256},{64,320},{128,384},{192,448},{256,0},{320,64},{384,128},{4... | collective-permute-start | bytes 207368 | tf_op jit(solution)/shard_map/ppermute | solution.py:324
  63.2 20.9 %collective-permute-start.8 = (f32[72,128]{1,0:T(8,128)S(1)}, f32[72,128]{1,0:T(8,128)S(1)}, u32[]{:S(2)}, u32[]{:S(2)}) collective-permute-start(f32[72,128]{1,0:T(8,128)S(1)} %get-tuple-element.22), channel_id=1, source_target_pairs={{0,63},{1,2},{2,1},{3,4},{4,3},{5,6},{6,5},{7,8},{8,7},{9,10},{10,... | collective-permute-start | bytes 110600 | tf_op jit(solution)/shard_map/ppermute | solution.py:326
  66.6 17.5 %collective-permute-start.7 = (f32[72,128]{1,0:T(8,128)S(1)}, f32[72,128]{1,0:T(8,128)S(1)}, u32[]{:S(2)}, u32[]{:S(2)}) collective-permute-start(f32[72,128]{1,0:T(8,128)S(1)} %get-tuple-element.22), channel_id=1, source_target_pairs={{0,1},{1,0},{2,3},{3,2},{4,5},{5,4},{6,7},{7,6},{8,9},{9,8},{10,11... | collective-permute-start | bytes 110600 | tf_op jit(solution)/shard_map/ppermute | solution.py:325
  72.1 21.8 %collective-permute-start.11 = (f32[135,128]{1,0:T(8,128)S(1)}, f32[135,128]{1,0:T(8,128)S(1)}, u32[]{:S(2)}, u32[]{:S(2)}) collective-permute-start(f32[135,128]{1,0:T(8,128)S(1)} %get-tuple-element.24), channel_id=1, source_target_pairs={{0,64},{64,128},{128,192},{192,0},{256,320},{320,384},{384,448},{4... | collective-permute-start | bytes 207368 | tf_op jit(solution)/shard_map/ppermute | solution.py:341
  75.6 18.4 %collective-permute-start.12 = (f32[135,128]{1,0:T(8,128)S(1)}, f32[135,128]{1,0:T(8,128)S(1)}, u32[]{:S(2)}, u32[]{:S(2)}) collective-permute-start(f32[135,128]{1,0:T(8,128)S(1)} %get-tuple-element.25), channel_id=1, source_target_pairs={{0,128},{64,192},{128,0},{192,64},{256,384},{320,448},{384,256},{4... | collective-permute-start | bytes 207368 | tf_op jit(solution)/shard_map/ppermute | solution.py:341
  80.2 13.8 %collective-permute-start.13 = (f32[135,128]{1,0:T(8,128)S(1)}, f32[135,128]{1,0:T(8,128)S(1)}, u32[]{:S(2)}, u32[]{:S(2)}) collective-permute-start(f32[135,128]{1,0:T(8,128)S(1)} %get-tuple-element.26), channel_id=1, source_target_pairs={{0,192},{64,0},{128,64},{192,128},{256,448},{320,256},{384,320},{4... | collective-permute-start | bytes 207368 | tf_op jit(solution)/shard_map/ppermute | solution.py:341
  84.2 9.8 %collective-permute-start.9 = (f32[72,128]{1,0:T(8,128)S(1)}, f32[72,128]{1,0:T(8,128)S(1)}, u32[]{:S(2)}, u32[]{:S(2)}) collective-permute-start(f32[72,128]{1,0:T(8,128)S(1)} %shard_map.133), channel_id=1, source_target_pairs={{0,32},{1,33},{2,34},{3,35},{4,36},{5,37},{6,38},{7,39},{8,40},{9,... | collective-permute-start | bytes 110600 | tf_op jit(solution)/shard_map/ppermute | solution.py:349
  (2 other events, 1.3 us)

commit v2 on v1

v2 whole, which is shorter than its diff:
```python
import functools
import math

import jax
import jax.numpy as jnp
import numpy as np
from jax import lax
from jax.experimental import pallas as pl
from jax.experimental.pallas import tpu as pltpu
from jax.sharding import PartitionSpec as P

SWEEPS = 2
LINE = (1.0 / 3.0, 4.0 / 3.0, 1.0 / 3.0)
VMEM = pl.BlockSpec(memory_space=pltpu.VMEM)
HBM = pl.BlockSpec(memory_space=pltpu.HBM)


def face_node(face, n):
    normal = face // 2
    tangent = [axis for axis in range(3) if axis != normal]
    coords = [0, 0, 0]
    coords[normal] = 2 * (face % 2)
    coords[tangent[0]] = n % 3
    coords[tangent[1]] = n // 3
    return 9 * coords[2] + 3 * coords[1] + coords[0]


NODE = [[face_node(face, n) for n in range(9)] for face in range(6)]
WEIGHT = [float(np.float32(LINE[n % 3] * LINE[n // 3])) for n in range(9)]


def coef_table(times):
    table = [0.0] * times
    for k in range(1, times):
        sign = (-1.0) ** k
        phase = math.pi * k / times
        table[k] = float(
            np.float32(0.3 * sign * math.cos(phase) / math.sin(phase) + 1.2 * sign / times)
        )
    return table


def split_rows(value):
    high = value.astype(jnp.bfloat16).astype(jnp.float32)
    return jnp.concatenate([high, value - high], axis=0).astype(jnp.bfloat16)


def join_rows(value):
    half = value.shape[0] // 2
    return value[:half] + value[half:]


def face_rows(x_ref):
    elems = x_ref.shape[1]
    pad = jnp.zeros((3, elems), jnp.float32)
    nodes = [
        jnp.concatenate([x_ref[pl.ds(m, 5, stride=27), :], pad], axis=0) for m in range(27)
    ]
    blocks = []
    for face in range(6):
        rows = jnp.concatenate([nodes[NODE[face][n]] * WEIGHT[n] for n in range(9)], axis=0)
        blocks.append(split_rows(rows))
    return jnp.concatenate(blocks, axis=1)


def onehot(code, elems):
    slots = code.shape[1]
    row = lax.broadcasted_iota(jnp.int32, (elems, slots), 0)
    parts = [
        jnp.where(row == code - face * elems, 1.0, 0.0).astype(jnp.bfloat16) for face in range(6)
    ]
    return jnp.concatenate(parts, axis=0)


def cross_code(elem_ref, face_ref, elems, order):
    code = face_ref[...] * elems + elem_ref[...]
    cap = code.shape[1] // 5
    parts = [code[:, k * cap : (k + 1) * cap] for k in order]
    fill = 256 - code.shape[1]
    return jnp.concatenate(parts + [jnp.full((1, fill), -1, jnp.int32)], axis=1)


def cross_trace(x_ref, hot, near_ref, far_ref):
    trace = join_rows(jnp.dot(face_rows(x_ref), hot, preferred_element_type=jnp.float32))
    near_ref[...] = trace[:, :128]
    far_ref[...] = trace[:, 128:]


def fetch(pairs, sems):
    copies = [
        pltpu.make_async_copy(source, target, sems.at[i])
        for i, (source, target) in enumerate(pairs)
    ]
    for copy in copies:
        copy.start()
    return copies


def first_kernel(
    start_ref, elem_hbm, face_hbm, x_ref, near_ref, far_ref, hot_ref, elem_ref, face_ref, sems
):
    copies = fetch(
        ((start_ref.at[:, 0], x_ref), (elem_hbm, elem_ref), (face_hbm, face_ref)), sems
    )
    for copy in copies[1:]:
        copy.wait()
    elems = x_ref.shape[1]
    hot_ref[...] = onehot(cross_code(elem_ref, face_ref, elems, (0, 4, 1, 2, 3)), elems)
    copies[0].wait()
    cross_trace(x_ref, hot_ref[...], near_ref, far_ref)


def received_rows(trace, orient, jacobian):
    slots = trace.shape[1]
    code = jnp.broadcast_to(orient, (8, slots))
    flip_i = (code & 1) == 1
    flip_j = ((code >> 1) & 1) == 1
    swap = code >= 4
    tile = [trace[8 * n : 8 * n + 8] for n in range(9)]
    for j in range(3):
        low, high = tile[3 * j], tile[3 * j + 2]
        tile[3 * j] = jnp.where(flip_i, high, low)
        tile[3 * j + 2] = jnp.where(flip_i, low, high)
    for i in range(3):
        low, high = tile[i], tile[6 + i]
        tile[i] = jnp.where(flip_j, high, low)
        tile[6 + i] = jnp.where(flip_j, low, high)
    for j in range(3):
        for i in range(j):
            one, two = tile[3 * j + i], tile[3 * i + j]
            tile[3 * j + i] = jnp.where(swap, two, one)
            tile[3 * i + j] = jnp.where(swap, one, two)
    rows = []
    for n in range(9):
        total = jacobian[0] * tile[n][0:1]
        for u in range(1, 5):
            total = total + jacobian[u] * tile[n][u : u + 1]
        rows.append(total)
    return jnp.concatenate(rows, axis=0)


def scatter_nodes(rows, hot, elems):
    placed = join_rows(
        lax.dot_general(
            split_rows(rows), hot, (((1,), (1,)), ((), ())), preferred_element_type=jnp.float32
        )
    )
    nodes = [None] * 27
    for face in range(6):
        for n in range(9):
            part = placed[8 * n : 8 * n + 8, face * elems : (face + 1) * elems]
            m = NODE[face][n]
            nodes[m] = part if nodes[m] is None else nodes[m] + part
    return nodes


def inner_sum(x_ref, hot, orient, jac_ref, out_ref):
    elems = x_ref.shape[1]
    half = hot.shape[1] // 2
    trace = join_rows(jnp.dot(face_rows(x_ref), hot, preferred_element_type=jnp.float32))
    trace = jnp.concatenate([trace[:, half:], trace[:, :half]], axis=1)
    jacobian = [jac_ref[8 * u : 8 * u + 8, :] for u in range(5)]
    nodes = scatter_nodes(received_rows(trace, orient, jacobian), hot, elems)
    for m in range(27):
        out_ref[8 * m : 8 * m + 8, :] = (
            nodes[m] if nodes[m] is not None else jnp.zeros((8, elems), jnp.float32)
        )


def prepare_kernel(
    cap,
    x_ref,
    elem_hbm,
    face_hbm,
    orient_hbm,
    jac_hbm,
    cross_elem_hbm,
    cross_face_hbm,
    cross_orient_hbm,
    count_hbm,
    cross_jac_hbm,
    source_hbm,
    mass_hbm,
    out_ref,
    hot_ref,
    turn_ref,
    jac_ref,
    cross_hot_ref,
    cross_turn_ref,
    cross_jac_ref,
    source_ref,
    mass_ref,
    elem_ref,
    face_ref,
    orient_ref,
    raw_ref,
    cross_elem_ref,
    cross_face_ref,
    cross_orient_ref,
    count_ref,
    cross_raw_ref,
    sems,
):
    copies = fetch(
        (
            (elem_hbm, elem_ref),
            (face_hbm, face_ref),
            (orient_hbm, orient_ref),
            (jac_hbm, raw_ref),
            (cross_elem_hbm, cross_elem_ref),
            (cross_face_hbm, cross_face_ref),
            (cross_orient_hbm, cross_orient_ref),
            (count_hbm, count_ref),
            (cross_jac_hbm, cross_raw_ref),
            (source_hbm.at[:, 0], source_ref),
            (mass_hbm, mass_ref),
        ),
        sems,
    )
    for copy in copies:
        copy.wait()
    elems = x_ref.shape[1]
    half = elem_ref.shape[1]
    code = face_ref[...] * elems + elem_ref[...]
    hot_ref[...] = onehot(jnp.concatenate([code[0:1], code[1:2]], axis=1), elems)
    orient = orient_ref[...]
    back = jnp.where(orient >= 4, 4 + 2 * (orient & 1) + ((orient >> 1) & 1), orient)
    turn_ref[...] = jnp.concatenate([orient, back], axis=1)
    jac_ref[...] = jnp.zeros_like(jac_ref)
    for u in range(5):
        for v in range(5):
            for side in range(2):
                jac_ref[8 * u + v : 8 * u + v + 1, side * half : (side + 1) * half] = raw_ref[
                    0, 5 * u + v, side : side + 1, :
                ]
    slots = 5 * cap
    fill = 256 - slots
    cross_hot_ref[...] = onehot(
        cross_code(cross_elem_ref, cross_face_ref, elems, range(5)), elems
    )
    cross_turn_ref[...] = jnp.concatenate(
        [cross_orient_ref[...], jnp.zeros((1, fill), jnp.int32)], axis=1
    )
    lane = lax.broadcasted_iota(jnp.int32, (1, slots), 1)
    count = count_ref[...]
    live = lane < 0
    for k in range(5):
        live = live | ((lane >= k * cap) & (lane - k * cap < count[:, k : k + 1]))
    cross_jac_ref[...] = jnp.zeros_like(cross_jac_ref)
    for u in range(5):
        for v in range(5):
            row = cross_raw_ref[5 * u + v]
            cross_jac_ref[8 * u + v : 8 * u + v + 1, :slots] = jnp.where(live, row, 0.0)
    inner_sum(x_ref, hot_ref[...], turn_ref[...], jac_ref, out_ref)


def inner_kernel(x_ref, hot_ref, turn_ref, jac_ref, out_ref):
    inner_sum(x_ref, hot_ref[...], turn_ref[...], jac_ref, out_ref)


def combine_kernel(times, x_ref, z_ref, out_ref):
    table = coef_table(times)
    half = times // 2
    y = lax.axis_index("tm") % half
    x = x_ref[...]
    z = z_ref[...] if len(z_ref.shape) == 2 else z_ref[:, 0, :]
    for target in range(half):
        own = jnp.float32(0.0)
        other = jnp.float32(0.0)
        for at in range(half):
            own = jnp.where(y == at, table[(at - target) % times], own)
            other = jnp.where(y == at, table[(at - target + half) % times], other)
        out_ref[target] = x * own + z * other


def relay_kernel(cap, even_ref, odd_ref, far_ref, out_ref):
    is_even = lax.axis_index("mesh") % 2 == 0
    even = even_ref[...]
    odd = odd_ref[...]
    above = jnp.where(is_even, even, odd)
    below = jnp.where(is_even, odd, even)
    out_ref[...] = jnp.concatenate(
        [far_ref[:, :cap], below[:, cap : 2 * cap], above[:, 3 * cap : 4 * cap], far_ref[:, :cap]],
        axis=1,
    )


def solve(held_ref, resid, out_ref, first, count):
    def body(step, carry):
        for r in range(5):
            i = first + step * 5 + r
            product = held_ref[0, i].astype(jnp.float32) * resid
            out_ref[pl.ds(i, 1), :] = jnp.sum(product, axis=0, keepdims=True)
        return carry

    lax.fori_loop(0, count // 5, body, 0)


def residual(
    cap,
    inner_ref,
    even_ref,
    odd_ref,
    far_ref,
    hot_ref,
    turn_ref,
    jac_ref,
    source_ref,
    mass_ref,
    terms_ref,
    resid_ref,
):
    elems = source_ref.shape[1]
    is_even = lax.axis_index("mesh") % 2 == 0
    even = even_ref[...]
    odd = odd_ref[...]
    far = far_ref[...]
    above = jnp.where(is_even, even, odd)
    below = jnp.where(is_even, odd, even)
    trace = jnp.concatenate(
        [
            above[:, 2 * cap : 3 * cap],
            below[:, :cap],
            far[:, cap : 2 * cap],
            far[:, :cap],
            far[:, 2 * cap : 3 * cap],
            jnp.zeros((72, 256 - 5 * cap), jnp.float32),
        ],
        axis=1,
    )
    jacobian = [jac_ref[8 * u : 8 * u + 8, :] for u in range(5)]
    nodes = scatter_nodes(received_rows(trace, turn_ref[...], jacobian), hot_ref[...], elems)
    for m in range(27):
        part = inner_ref[8 * m : 8 * m + 8, :]
        part = part if nodes[m] is None else part + nodes[m]
        resid_ref[pl.ds(m, 5, stride=27), :] = part[:5]
    spectral = (terms_ref[0] + terms_ref[1]) + (terms_ref[2] + terms_ref[3])
    resid = source_ref[...] - resid_ref[...] - mass_ref[...] * spectral
    return resid.astype(jnp.bfloat16).astype(jnp.float32)


def middle_kernel(cap, *refs):
    *operands, held_ref, send_ref, out_ref, near_ref, far_ref, resid_ref = refs
    resid = residual(cap, *operands, resid_ref)
    solve(held_ref, resid, out_ref, 0, held_ref.shape[1])
    cross_trace(out_ref, send_ref[...], near_ref, far_ref)


def last_kernel(cap, *refs):
    *operands, held_ref, result_ref, resid_ref, out_ref, sems = refs
    resid = residual(cap, *operands, resid_ref)
    per = held_ref.shape[1] // 3
    copies = []
    for c in range(3):
        solve(held_ref, resid, out_ref, c * per, per)
        copy = pltpu.make_async_copy(
            out_ref.at[pl.ds(c * per, per)], result_ref.at[pl.ds(c * per, per), 0], sems.at[c]
        )
        copy.start()
        copies.append(copy)
    for copy in copies:
        copy.wait()


def on_device(
    inverse,
    start,
    source,
    mass,
    inner_elem,
    inner_face,
    inner_orient,
    inner_jac,
    cross_elem,
    cross_face,
    cross_orient,
    cross_count,
    cross_jac,
):
    size, elems = start.shape[1:]
    count_mesh = lax.axis_size("mesh")
    times = lax.axis_size("tm")
    half_times = times // 2
    cap = cross_elem.shape[1] // 5
    faces = inner_elem.shape[1]
    f32, i32, bf16 = jnp.float32, jnp.int32, jnp.bfloat16

    def struct(shape, dtype=f32):
        return jax.ShapeDtypeStruct(shape, dtype)

    state = struct((size, elems))
    near_shape = struct((72, 128))
    hot_cross = struct((6 * elems, 256), bf16)
    params = pltpu.CompilerParams(vmem_limit_bytes=16 * 1024 * 1024)
    dma = pltpu.SemaphoreType.DMA
    cost = pl.CostEstimate(flops=4000000000, bytes_accessed=1000000, transcendentals=0)

    across = [(t, (t + half_times) % times) for t in range(times)]
    halves = [list(range(half_times)), list(range(half_times, times))]
    evens = [(p, p ^ 1) for p in range(count_mesh)]
    odds = [(p, (((p + 1) ^ 1) - 1) % count_mesh) for p in range(count_mesh)]
    opposite = [(p, (p + count_mesh // 2) % count_mesh) for p in range(count_mesh)]

    start_rows = start.transpose(1, 0, 2)
    over = lax.ppermute(start_rows, "tm", across)
    x, near, far, send_hot = pl.pallas_call(
        first_kernel,
        out_shape=(state, near_shape, near_shape, hot_cross),
        in_specs=[HBM] * 3,
        out_specs=(VMEM,) * 4,
        scratch_shapes=[
            pltpu.VMEM(cross_elem.shape, i32),
            pltpu.VMEM(cross_face.shape, i32),
            dma((3,)),
        ],
        compiler_params=params,
    )(start_rows, cross_elem, cross_face)
    even = lax.ppermute(near, "mesh", evens)
    odd = lax.ppermute(near, "mesh", odds)
    jac_rows = inner_jac.transpose(0, 2, 1, 3)
    cross_rows = cross_jac[0]
    prepare = pl.pallas_call(
        functools.partial(prepare_kernel, cap),
        out_shape=(
            struct((216, elems)),
            struct((6 * elems, 2 * faces), bf16),
            struct((1, 2 * faces), i32),
            struct((40, 2 * faces)),
            hot_cross,
            struct((1, 256), i32),
            struct((40, 256)),
            state,
            state,
        ),
        in_specs=[VMEM] + [HBM] * 11,
        out_specs=(VMEM,) * 9,
        scratch_shapes=[
            pltpu.VMEM(inner_elem.shape, i32),
            pltpu.VMEM(inner_face.shape, i32),
            pltpu.VMEM((1, faces), i32),
            pltpu.VMEM(jac_rows.shape, f32),
            pltpu.VMEM(cross_elem.shape, i32),
            pltpu.VMEM(cross_face.shape, i32),
            pltpu.VMEM(cross_orient.shape, i32),
            pltpu.VMEM(cross_count.shape, i32),
            pltpu.VMEM(cross_rows.shape, f32),
            dma((11,)),
        ],
        compiler_params=params,
        cost_estimate=cost,
    )
    for sweep in range(SWEEPS):
        last = sweep == SWEEPS - 1
        if sweep > 0:
            over = lax.ppermute(x, "tm", across)
            even = lax.ppermute(near, "mesh", evens)
            odd = lax.ppermute(near, "mesh", odds)
        passed = pl.pallas_call(
            functools.partial(relay_kernel, cap),
            out_shape=near_shape,
            in_specs=[VMEM] * 3,
            out_specs=VMEM,
            compiler_params=params,
        )(even, odd, far)
        over, _ = lax.optimization_barrier((over, passed))
        terms = pl.pallas_call(
            functools.partial(combine_kernel, times),
            out_shape=struct((half_times, size, elems)),
            in_specs=[VMEM] * 2,
            out_specs=VMEM,
            compiler_params=params,
            cost_estimate=cost,
        )(x, over)
        passed = lax.ppermute(passed, "mesh", opposite)
        x, _ = lax.optimization_barrier((x, terms))
        if sweep > 0:
            inner = pl.pallas_call(
                inner_kernel,
                out_shape=struct((216, elems)),
                in_specs=[VMEM] * 4,
                out_specs=VMEM,
                compiler_params=params,
                cost_estimate=cost,
            )(x, hot, turn, jac)
        else:
            inner, hot, turn, jac, *tables = prepare(
                x,
                inner_elem,
                inner_face,
                inner_orient[None, :],
                jac_rows,
                cross_elem,
                cross_face,
                cross_orient,
                cross_count,
                cross_rows,
                source.transpose(1, 0, 2),
                mass,
            )
        terms = lax.all_to_all(
            terms, "tm", split_axis=0, concat_axis=0, tiled=True, axis_index_groups=halves
        )
        operands = (inner, even, odd, passed, *tables, terms, inverse)
        if last:
            out = pl.pallas_call(
                functools.partial(last_kernel, cap),
                out_shape=struct((size, 1, elems)),
                in_specs=[VMEM] * 11,
                out_specs=HBM,
                scratch_shapes=[
                    pltpu.VMEM((size, elems), f32),
                    pltpu.VMEM((size, elems), f32),
                    dma((3,)),
                ],
                compiler_params=params,
            )(*operands)
            return out.transpose(1, 0, 2)
        x, near, far = pl.pallas_call(
            functools.partial(middle_kernel, cap),
            out_shape=(state, near_shape, near_shape),
            in_specs=[VMEM] * 12,
            out_specs=(VMEM,) * 3,
            scratch_shapes=[pltpu.VMEM((size, elems), f32)],
            compiler_params=params,
        )(*operands, send_hot)


def solution(mesh):
    in_specs = (
        P("tm", None, None, "mesh"),
        P("tm", None, "mesh"),
        P("tm", None, "mesh"),
        P(None, "mesh"),
        P(None, "mesh"),
        P(None, "mesh"),
        P("mesh"),
        P("tm", None, None, "mesh"),
        P("mesh", None),
        P("mesh", None),
        P("mesh", None),
        P("mesh", None),
        P("tm", None, "mesh", None),
    )
    out_specs = P("tm", None, "mesh")
    return jax.shard_map(
        on_device, mesh=mesh, in_specs=in_specs, out_specs=out_specs, check_vma=False
    )
```

time: 101 us -> 87 us (0.86)
  the two profiles are of different devices: /device:TPU:16 before, /device:TPU:24 now
where the time goes in v2:
time: 87 us; the launch traced here: 85.6 us
  starting transfers between devices  52.6 us (60%)
  waiting for transfers between devices  16.8 us (19%)
  Pallas kernels  8.88 us (10%)
  local copies, waits for them, and re-layouts  6.98 us (8%)
    ppermute x1, starting transfers between devices, on_device(): over = lax.ppermute(start_rows, 'tm', across)  15.7 us
    ppermute x2, starting transfers between devices, on_device(): odd = lax.ppermute(near, 'mesh', odds)  14.7 us
    all_to_all x2, starting transfers between devices, on_device(): lax.all_to_all(terms, 'tm', split_axis=0, concat_axis=0, tiled=True, axis...  10.2 us
    ppermute x2, waiting for transfers between devices, on_device(): odd = lax.ppermute(near, 'mesh', odds)  9.48 us
    unnamed x32, local copies, waits for them, and re-layouts  6.98 us
    all_to_all x2, waiting for transfers between devices, on_device(): lax.all_to_all(terms, 'tm', split_axis=0, concat_axis=0, tiled=True, axis...  6.19 us
    ppermute x2, starting transfers between devices, on_device(): passed = lax.ppermute(passed, 'mesh', opposite)  4.27 us
    ppermute x1, starting transfers between devices, on_device(): over = lax.ppermute(x, 'tm', across)  3.93 us
  transfers between devices with their start and end apart: 10, of which 6 were waited for; matrix products, arithmetic and copies ran while one was open for 0% of the time, Pallas kernels for 5%

profile of v2, /device:TPU:24, one launch (start us, length us, event | category | flops | bytes accessed | tf_op | source)
XLA Modules:
  0.0 85.6 jit_solution(13987336840259646621)
XLA Ops:
  0.0 15.7 %collective-permute-start = (f32[135,1,128]{2,1,0:T(1,128)}, f32[135,1,128]{2,1,0:T(1,128)S(1)}, u32[]{:S(2)}, u32[]{:S(2)}) collective-permute-start(f32[135,1,128]{2,1,0:T(1,128)} %bitcast.6), channel_id=1, source_target_pairs={{0,256},{64,320},{128,384},{192,448},{256,0},{320,64},{384,128},{4... | collective-permute-start | bytes 207368 | tf_op jit(solution)/shard_map/ppermute | solution.py:405
  15.7 0.9 %copy-done.2 = f32[1,135,128]{2,0,1:T(1,128)S(1)} copy-done((f32[1,135,128]{2,0,1:T(1,128)S(1)}, f32[1,135,128]{2,0,1:T(1,128)}, u32[]{:S(2)}) %copy-start.2) | copy-done | bytes 69144
  16.6 0.7 copy-done.3
  18.5 7.0 %collective-permute-start.2 = (f32[72,128]{1,0:T(8,128)S(1)}, f32[72,128]{1,0:T(8,128)S(1)}, u32[]{:S(2)}, u32[]{:S(2)}) collective-permute-start(f32[72,128]{1,0:T(8,128)S(1)} %get-tuple-element.26), channel_id=1, source_target_pairs={{0,63},{1,2},{2,1},{3,4},{4,3},{5,6},{6,5},{7,8},{8,7},{9,10},{10,... | collective-permute-start | bytes 110600 | tf_op jit(solution)/shard_map/ppermute | solution.py:419
  25.5 1.9 %collective-permute-start.1 = (f32[72,128]{1,0:T(8,128)S(1)}, f32[72,128]{1,0:T(8,128)S(1)}, u32[]{:S(2)}, u32[]{:S(2)}) collective-permute-start(f32[72,128]{1,0:T(8,128)S(1)} %get-tuple-element.26), channel_id=1, source_target_pairs={{0,1},{1,0},{2,3},{3,2},{4,5},{5,4},{6,7},{7,6},{8,9},{9,8},{10,11... | collective-permute-start | bytes 110600 | tf_op jit(solution)/shard_map/ppermute | solution.py:418
  27.5 5.0 %collective-permute-done.2.odd_ref.refs_2_ = f32[72,128]{1,0:T(8,128)S(1)} collective-permute-done((f32[72,128]{1,0:T(8,128)S(1)}, f32[72,128]{1,0:T(8,128)S(1)}, u32[]{:S(2)}, u32[]{:S(2)}) %collective-permute-start.2) | collective-permute-done | bytes 36896 | tf_op jit(solution)/shard_map/ppermute | solution.py:419
  32.6 1.9 %collective-permute-start.3 = (f32[72,128]{1,0:T(8,128)S(1)}, f32[72,128]{1,0:T(8,128)S(1)}, u32[]{:S(2)}, u32[]{:S(2)}) collective-permute-start(f32[72,128]{1,0:T(8,128)S(1)} %shard_map.128), channel_id=1, source_target_pairs={{0,32},{1,33},{2,34},{3,35},{4,36},{5,37},{6,38},{7,39},{8,40},{9,... | collective-permute-start | bytes 110600 | tf_op jit(solution)/shard_map/ppermute | solution.py:474
  34.7 0.9 %shard_map.129 = f32[4,135,128]{2,1,0:T(8,128)} custom-call(f32[135,128]{1,0:T(8,128)S(1)} %get-tuple-element.29.x_ref, f32[135,1,128]{2,1,0:T(1,128)S(1)} %collective-permute-done.z_ref), custom_call_target="tpu_custom_call" | custom-call | flops 4000000000 | bytes 1000000 | tf_op jit(solution)/shard_map/pallas_call | solution.py:466
  35.6 4.7 %all-to-all-start = ((f32[4,135,128]{2,1,0:T(8,128)}), f32[4,135,128]{2,1,0:T(8,128)S(1)}, u32[]{:S(2)}, u32[]{:S(2)}) async-start(f32[4,135,128]{2,1,0:T(8,128)} %shard_map.129), calls=%async_computation | async-start | bytes 557056 | tf_op jit(solution)/shard_map/all_to_all | solution.py:500
  40.4 1.3 %shard_map.130 = (f32[216,128]{1,0:T(8,128)S(1)}, bf16[768,512]{1,0:T(8,128)(2,1)S(1)}, s32[1,512]{1,0:T(1,128)S(1)}, f32[40,512]{1,0:T(8,128)S(1)}, bf16[768,25...) custom-call(f32[135,128]{1,0:T(8,128)S(1)} %get-tuple-element.29.x_r, ...), custom_call_target="tpu_custom_call" | custom-call | flops 4000000000 | bytes 1000000 | tf_op jit(solution)/shard_map/pallas_call | solution.py:486
  42.4 2.6 %all-to-all-done.refs_9_ = f32[4,135,128]{2,1,0:T(8,128)S(1)} async-done(((f32[4,135,128]{2,1,0:T(8,128)}), f32[4,135,128]{2,1,0:T(8,128)S(1)}, u32[]{:S(2)}, u32[]{:S(2)}) %all-to-all-start) | async-done | bytes 276512 | tf_op jit(solution)/shard_map/all_to_all | solution.py:500
  45.0 2.3 %copy-done = bf16[1,135,135,128]{3,2,1,0:T(8,128)(2,1)S(1)} copy-done((bf16[1,135,135,128]{3,2,1,0:T(8,128)(2,1)S(1)}, bf16[1,135,135,128]{3,2,1,0:T(8,128)(2,1)}, u32[]{:S(2)}) %copy-start) | copy-done | bytes 4665624
  47.3 2.1 %shard_map.131 = (f32[135,128]{1,0:T(8,128)S(1)}, f32[72,128]{1,0:T(8,128)S(1)}, f32[72,128]{1,0:T(8,128)S(1)}) custom-call(f32[216,128]{1,0:T(8,128)S(1)} %get-tuple-element.30.refs_0_, f32[72,128]{1,0:T(8,128)S(1)} %collective-permute-done.1.even_ref.refs_1_, f32[72,128]{1,0:T(8,128)S(1)} %collective-permute-done.2.odd_ref.refs_2_, ...), custom_call_target="tpu_custom_call" | custom-call | tf_op jit(solution)/shard_map/pallas_call | solution.py:518
  49.4 3.9 %collective-permute-start.4 = (f32[135,128]{1,0:T(8,128)S(1)}, f32[135,128]{1,0:T(8,128)S(1)}, u32[]{:S(2)}, u32[]{:S(2)}) collective-permute-start(f32[135,128]{1,0:T(8,128)S(1)} %get-tuple-element.41.x_ref), channel_id=1, source_target_pairs={{0,256},{64,320},{128,384},{192,448},{256,0},{320,64},{384,128},{4... | collective-permute-start | bytes 207368 | tf_op jit(solution)/shard_map/ppermute | solution.py:455
  53.3 7.7 %collective-permute-start.6 = (f32[72,128]{1,0:T(8,128)S(1)}, f32[72,128]{1,0:T(8,128)S(1)}, u32[]{:S(2)}, u32[]{:S(2)}) collective-permute-start(f32[72,128]{1,0:T(8,128)S(1)} %get-tuple-element.38), channel_id=1, source_target_pairs={{0,63},{1,2},{2,1},{3,4},{4,3},{5,6},{6,5},{7,8},{8,7},{9,10},{10,... | collective-permute-start | bytes 110600 | tf_op jit(solution)/shard_map/ppermute | solution.py:457
  61.0 1.9 %collective-permute-start.5 = (f32[72,128]{1,0:T(8,128)S(1)}, f32[72,128]{1,0:T(8,128)S(1)}, u32[]{:S(2)}, u32[]{:S(2)}) collective-permute-start(f32[72,128]{1,0:T(8,128)S(1)} %get-tuple-element.38), channel_id=1, source_target_pairs={{0,1},{1,0},{2,3},{3,2},{4,5},{5,4},{6,7},{7,6},{8,9},{9,8},{10,11... | collective-permute-start | bytes 110600 | tf_op jit(solution)/shard_map/ppermute | solution.py:456
  63.0 4.4 %collective-permute-done.6.odd_ref.refs_2_ = f32[72,128]{1,0:T(8,128)S(1)} collective-permute-done((f32[72,128]{1,0:T(8,128)S(1)}, f32[72,128]{1,0:T(8,128)S(1)}, u32[]{:S(2)}, u32[]{:S(2)}) %collective-permute-start.6) | collective-permute-done | bytes 36896 | tf_op jit(solution)/shard_map/ppermute | solution.py:457
  67.5 2.4 %collective-permute-start.7 = (f32[72,128]{1,0:T(8,128)S(1)}, f32[72,128]{1,0:T(8,128)S(1)}, u32[]{:S(2)}, u32[]{:S(2)}) collective-permute-start(f32[72,128]{1,0:T(8,128)S(1)} %shard_map.132), channel_id=1, source_target_pairs={{0,32},{1,33},{2,34},{3,35},{4,36},{5,37},{6,38},{7,39},{8,40},{9,... | collective-permute-start | bytes 110600 | tf_op jit(solution)/shard_map/ppermute | solution.py:474
  69.9 0.8 shard_map.133
  70.6 5.5 %all-to-all-start.1 = ((f32[4,135,128]{2,1,0:T(8,128)}), f32[4,135,128]{2,1,0:T(8,128)S(1)}, u32[]{:S(2)}, u32[]{:S(2)}) async-start(f32[4,135,128]{2,1,0:T(8,128)} %shard_map.133), calls=%async_computation.1 | async-start | bytes 557056 | tf_op jit(solution)/shard_map/all_to_all | solution.py:500
  76.1 0.7 shard_map.134.refs_0_
  77.3 3.6 %all-to-all-done.1.refs_9_ = f32[4,135,128]{2,1,0:T(8,128)S(1)} async-done(((f32[4,135,128]{2,1,0:T(8,128)}), f32[4,135,128]{2,1,0:T(8,128)S(1)}, u32[]{:S(2)}, u32[]{:S(2)}) %all-to-all-start.1) | async-done | bytes 276512 | tf_op jit(solution)/shard_map/all_to_all | solution.py:500
  80.8 2.3 %copy-done.1 = bf16[1,135,135,128]{3,2,1,0:T(8,128)(2,1)S(1)} copy-done((bf16[1,135,135,128]{3,2,1,0:T(8,128)(2,1)S(1)}, bf16[1,135,135,128]{3,2,1,0:T(8,128)(2,1)}, u32[]{:S(2)}) %copy-start.1) | copy-done | bytes 4665624
  83.2 2.4 %shard_map.135 = f32[135,1,128]{2,1,0:T(1,128)} custom-call(f32[216,128]{1,0:T(8,128)S(1)} %shard_map.134.refs_0_, f32[72,128]{1,0:T(8,128)S(1)} %collective-permute-done.5.even_ref.refs_1_, f32[72,128]{1,0:T(8,128)S(1)} %collective-permute-done.6.odd_ref.refs_2_, f32[72,128]{1,0:T(8,128)S(1)} %collective-permute-done.7.refs_3_, ...), custom_call_target="tpu_custom_call" | custom-call | tf_op jit(solution)/shard_map/pallas_call | solution.py:505
  (37 shorter events, 2.6 us)
Async XLA Ops:
  0.0 34.5 %collective-permute-start = (f32[135,1,128]{2,1,0:T(1,128)}, f32[135,1,128]{2,1,0:T(1,128)S(1)}, u32[]{:S(2)}, u32[]{:S(2)}) collective-permute-start(f32[135,1,128]{2,1,0:T(1,128)} %bitcast.6), channel_id=1, source_target_pairs={{0,256},{64,320},{128,384},{192,448},{256,0},{320,64},{384,128},{4... | collective-permute-start | bytes 207368 | tf_op jit(solution)/shard_map/ppermute | solution.py:405
  15.7 0.9 %copy-start.2 = (f32[1,135,128]{2,0,1:T(1,128)S(1)}, f32[1,135,128]{2,0,1:T(1,128)}, u32[]{:S(2)}) copy-start(f32[1,135,128]{2,0,1:T(1,128)} %param.14) | copy-start | bytes 207364
  18.5 14.0 %collective-permute-start.2 = (f32[72,128]{1,0:T(8,128)S(1)}, f32[72,128]{1,0:T(8,128)S(1)}, u32[]{:S(2)}, u32[]{:S(2)}) collective-permute-start(f32[72,128]{1,0:T(8,128)S(1)} %get-tuple-element.26), channel_id=1, source_target_pairs={{0,63},{1,2},{2,1},{3,4},{4,3},{5,6},{6,5},{7,8},{8,7},{9,10},{10,... | collective-permute-start | bytes 110600 | tf_op jit(solution)/shard_map/ppermute | solution.py:419
  25.5 7.0 %collective-permute-start.1 = (f32[72,128]{1,0:T(8,128)S(1)}, f32[72,128]{1,0:T(8,128)S(1)}, u32[]{:S(2)}, u32[]{:S(2)}) collective-permute-start(f32[72,128]{1,0:T(8,128)S(1)} %get-tuple-element.26), channel_id=1, source_target_pairs={{0,1},{1,0},{2,3},{3,2},{4,5},{5,4},{6,7},{7,6},{8,9},{9,8},{10,11... | collective-permute-start | bytes 110600 | tf_op jit(solution)/shard_map/ppermute | solution.py:418
  32.6 9.8 %collective-permute-start.3 = (f32[72,128]{1,0:T(8,128)S(1)}, f32[72,128]{1,0:T(8,128)S(1)}, u32[]{:S(2)}, u32[]{:S(2)}) collective-permute-start(f32[72,128]{1,0:T(8,128)S(1)} %shard_map.128), channel_id=1, source_target_pairs={{0,32},{1,33},{2,34},{3,35},{4,36},{5,37},{6,38},{7,39},{8,40},{9,... | collective-permute-start | bytes 110600 | tf_op jit(solution)/shard_map/ppermute | solution.py:474
  34.5 5.8 %copy-start.4 = (s32[1,160]{1,0:T(1,128)S(1)}, s32[1,160]{1,0:T(1,128)}, u32[]{:S(2)}) copy-start(s32[1,160]{1,0:T(1,128)} %cross_elem_hbm.1) | copy-start | bytes 1924
  34.5 5.8 %copy-start.6 = (s32[1,160]{1,0:T(1,128)S(1)}, s32[1,160]{1,0:T(1,128)}, u32[]{:S(2)}) copy-start(s32[1,160]{1,0:T(1,128)} %cross_face_hbm.1) | copy-start | bytes 1924
  34.6 5.7 %copy-start.7 = (f32[135,128]{1,0:T(8,128)S(1)}, f32[135,128]{1,0:T(8,128)}, u32[]{:S(2)}) copy-start(f32[135,128]{1,0:T(8,128)} %mass_hbm.1) | copy-start | bytes 207364
  34.6 5.7 %copy-start.8 = (f32[1,135,128]{2,0,1:T(1,128)S(1)}, f32[1,135,128]{2,0,1:T(1,128)}, u32[]{:S(2)}) copy-start(f32[1,135,128]{2,0,1:T(1,128)} %param.15) | copy-start | bytes 207364
  34.6 5.7 %copy-start.9 = (f32[1,2,25,256]{3,1,2,0:T(2,128)S(1)}, f32[1,2,25,256]{3,1,2,0:T(2,128)}, u32[]{:S(2)}) copy-start(f32[1,2,25,256]{3,1,2,0:T(2,128)} %param.20) | copy-start | bytes 153604
  34.6 5.7 %copy-start.10 = (f32[1,25,1,160]{3,2,1,0:T(1,128)S(1)}, f32[1,25,1,160]{3,2,1,0:T(1,128)}, u32[]{:S(2)}) copy-start(f32[1,25,1,160]{3,2,1,0:T(1,128)} %param.25) | copy-start | bytes 48004
  34.6 5.7 %copy-start.11 = (s32[2,256]{1,0:T(2,128)S(1)}, s32[2,256]{1,0:T(2,128)}, u32[]{:S(2)}) copy-start(s32[2,256]{1,0:T(2,128)} %elem_hbm.3) | copy-start | bytes 6148
  34.6 5.7 %copy-start.12 = (s32[2,256]{1,0:T(2,128)S(1)}, s32[2,256]{1,0:T(2,128)}, u32[]{:S(2)}) copy-start(s32[2,256]{1,0:T(2,128)} %face_hbm.3) | copy-start | bytes 6148
  34.6 5.7 %copy-start.13 = (s32[256]{0:T(256)S(1)}, s32[256]{0:T(256)}, u32[]{:S(2)}) copy-start(s32[256]{0:T(256)} %param.19) | copy-start | bytes 3076
  34.6 5.7 %copy-start.14 = (s32[1,160]{1,0:T(1,128)S(1)}, s32[1,160]{1,0:T(1,128)}, u32[]{:S(2)}) copy-start(s32[1,160]{1,0:T(1,128)} %cross_orient_hbm.1) | copy-start | bytes 1924
  34.7 5.7 %copy-start.15 = (s32[1,5]{1,0:T(1,128)S(1)}, s32[1,5]{1,0:T(1,128)}, u32[]{:S(2)}) copy-start(s32[1,5]{1,0:T(1,128)} %count_hbm.1) | copy-start | bytes 64
  35.6 9.4 %all-to-all-start = ((f32[4,135,128]{2,1,0:T(8,128)}), f32[4,135,128]{2,1,0:T(8,128)S(1)}, u32[]{:S(2)}, u32[]{:S(2)}) async-start(f32[4,135,128]{2,1,0:T(8,128)} %shard_map.129), calls=%async_computation | async-start | bytes 557056 | tf_op jit(solution)/shard_map/all_to_all | solution.py:500
  45.0 2.3 %copy-start = (bf16[1,135,135,128]{3,2,1,0:T(8,128)(2,1)S(1)}, bf16[1,135,135,128]{3,2,1,0:T(8,128)(2,1)}, u32[]{:S(2)}) copy-start(bf16[1,135,135,128]{3,2,1,0:T(8,128)(2,1)} %refs_10_.3) | copy-start | bytes 13996804
  49.4 20.5 %collective-permute-start.4 = (f32[135,128]{1,0:T(8,128)S(1)}, f32[135,128]{1,0:T(8,128)S(1)}, u32[]{:S(2)}, u32[]{:S(2)}) collective-permute-start(f32[135,128]{1,0:T(8,128)S(1)} %get-tuple-element.41.x_ref), channel_id=1, source_target_pairs={{0,256},{64,320},{128,384},{192,448},{256,0},{320,64},{384,128},{4... | collective-permute-start | bytes 207368 | tf_op jit(solution)/shard_map/ppermute | solution.py:455
  53.3 14.1 %collective-permute-start.6 = (f32[72,128]{1,0:T(8,128)S(1)}, f32[72,128]{1,0:T(8,128)S(1)}, u32[]{:S(2)}, u32[]{:S(2)}) collective-permute-start(f32[72,128]{1,0:T(8,128)S(1)} %get-tuple-element.38), channel_id=1, source_target_pairs={{0,63},{1,2},{2,1},{3,4},{4,3},{5,6},{6,5},{7,8},{8,7},{9,10},{10,... | collective-permute-start | bytes 110600 | tf_op jit(solution)/shard_map/ppermute | solution.py:457
  61.0 6.4 %collective-permute-start.5 = (f32[72,128]{1,0:T(8,128)S(1)}, f32[72,128]{1,0:T(8,128)S(1)}, u32[]{:S(2)}, u32[]{:S(2)}) collective-permute-start(f32[72,128]{1,0:T(8,128)S(1)} %get-tuple-element.38), channel_id=1, source_target_pairs={{0,1},{1,0},{2,3},{3,2},{4,5},{5,4},{6,7},{7,6},{8,9},{9,8},{10,11... | collective-permute-start | bytes 110600 | tf_op jit(solution)/shard_map/ppermute | solution.py:456
  67.5 9.8 %collective-permute-start.7 = (f32[72,128]{1,0:T(8,128)S(1)}, f32[72,128]{1,0:T(8,128)S(1)}, u32[]{:S(2)}, u32[]{:S(2)}) collective-permute-start(f32[72,128]{1,0:T(8,128)S(1)} %shard_map.132), channel_id=1, source_target_pairs={{0,32},{1,33},{2,34},{3,35},{4,36},{5,37},{6,38},{7,39},{8,40},{9,... | collective-permute-start | bytes 110600 | tf_op jit(solution)/shard_map/ppermute | solution.py:474
  70.6 10.2 %all-to-all-start.1 = ((f32[4,135,128]{2,1,0:T(8,128)}), f32[4,135,128]{2,1,0:T(8,128)S(1)}, u32[]{:S(2)}, u32[]{:S(2)}) async-start(f32[4,135,128]{2,1,0:T(8,128)} %shard_map.133), calls=%async_computation.1 | async-start | bytes 557056 | tf_op jit(solution)/shard_map/all_to_all | solution.py:500
  80.8 2.3 %copy-start.1 = (bf16[1,135,135,128]{3,2,1,0:T(8,128)(2,1)S(1)}, bf16[1,135,135,128]{3,2,1,0:T(8,128)(2,1)}, u32[]{:S(2)}) copy-start(bf16[1,135,135,128]{3,2,1,0:T(8,128)(2,1)} %refs_10_.3) | copy-start | bytes 13996804
  (2 other events, 1.4 us)

commit v3 on v2

--- a/solution.py
+++ b/solution.py
@@ -96,8 +96,16 @@
     return copies
 
 
+def tick_kernel(out_ref):
+    out_ref[...] = jnp.zeros_like(out_ref)
+
+
+def mark_kernel(x_ref, out_ref):
+    out_ref[...] = x_ref[:8]
+
+
 def first_kernel(
-    start_ref, elem_hbm, face_hbm, x_ref, near_ref, far_ref, hot_ref, elem_ref, face_ref, sems
+    tick_ref, start_ref, elem_hbm, face_hbm, x_ref, near_ref, far_ref, hot_ref, elem_ref, face_ref, sems
 ):
     copies = fetch(
         ((start_ref.at[:, 0], x_ref), (elem_hbm, elem_ref), (face_hbm, face_ref)), sems
@@ -273,14 +281,31 @@
         out_ref[target] = x * own + z * other
 
 
-def relay_kernel(cap, even_ref, odd_ref, far_ref, out_ref):
-    is_even = lax.axis_index("mesh") % 2 == 0
+def relay_kernel(cap, even_ref, odd_ref, near_ref, far_ref, out_ref):
+    part = lax.axis_index("mesh")
+    half = lax.axis_size("mesh") // 2
+    is_even = part % 2 == 0
     even = even_ref[...]
     odd = odd_ref[...]
     above = jnp.where(is_even, even, odd)
     below = jnp.where(is_even, odd, even)
+    one = jnp.where(
+        part % half == 0, near_ref[:, 2 * cap : 3 * cap], below[:, cap : 2 * cap]
+    )
+    two = jnp.where(
+        part % half == half - 1, near_ref[:, :cap], above[:, 3 * cap : 4 * cap]
+    )
+    out_ref[...] = jnp.concatenate([far_ref[:, :cap], one, two, two], axis=1)
+
+
+def forward_kernel(cap, near_ref, far_ref, out_ref):
     out_ref[...] = jnp.concatenate(
-        [far_ref[:, :cap], below[:, cap : 2 * cap], above[:, 3 * cap : 4 * cap], far_ref[:, :cap]],
+        [
+            near_ref[:, cap : 2 * cap],
+            near_ref[:, 3 * cap : 4 * cap],
+            far_ref[:, cap : 2 * cap],
+            far_ref[:, 2 * cap : 3 * cap],
+        ],
         axis=1,
     )
 
@@ -302,6 +327,7 @@
     even_ref,
     odd_ref,
     far_ref,
+    edge_ref,
     hot_ref,
     turn_ref,
     jac_ref,
@@ -311,19 +337,24 @@
     resid_ref,
 ):
     elems = source_ref.shape[1]
-    is_even = lax.axis_index("mesh") % 2 == 0
+    part = lax.axis_index("mesh")
+    half = lax.axis_size("mesh") // 2
+    is_even = part % 2 == 0
+    first = part % half == 0
+    final = part % half == half - 1
     even = even_ref[...]
     odd = odd_ref[...]
     far = far_ref[...]
+    edge = edge_ref[...]
     above = jnp.where(is_even, even, odd)
     below = jnp.where(is_even, odd, even)
     trace = jnp.concatenate(
         [
-            above[:, 2 * cap : 3 * cap],
-            below[:, :cap],
-            far[:, cap : 2 * cap],
+            jnp.where(final, edge[:, 2 * cap : 3 * cap], above[:, 2 * cap : 3 * cap]),
+            jnp.where(first, edge[:, 3 * cap : 4 * cap], below[:, :cap]),
+            jnp.where(first, edge[:, :cap], far[:, cap : 2 * cap]),
             far[:, :cap],
-            far[:, 2 * cap : 3 * cap],
+            jnp.where(final, edge[:, cap : 2 * cap], far[:, 2 * cap : 3 * cap]),
             jnp.zeros((72, 256 - 5 * cap), jnp.float32),
         ],
         axis=1,
@@ -398,15 +429,33 @@
     across = [(t, (t + half_times) % times) for t in range(times)]
     halves = [list(range(half_times)), list(range(half_times, times))]
     evens = [(p, p ^ 1) for p in range(count_mesh)]
-    odds = [(p, (((p + 1) ^ 1) - 1) % count_mesh) for p in range(count_mesh)]
+    half_mesh = count_mesh // 2
+    odds = [
+        (p, ((p + 1) ^ 1) - 1)
+        for p in range(count_mesh)
+        if p % half_mesh not in (0, half_mesh - 1)
+    ]
+    edges = [
+        (p, p // half_mesh * half_mesh + half_mesh - 1 - p % half_mesh)
+        for p in range(count_mesh)
+        if p % half_mesh in (0, half_mesh - 1)
+    ]
     opposite = [(p, (p + count_mesh // 2) % count_mesh) for p in range(count_mesh)]
 
     start_rows = start.transpose(1, 0, 2)
-    over = lax.ppermute(start_rows, "tm", across)
+    tick = pl.pallas_call(
+        tick_kernel,
+        out_shape=struct((8, 128)),
+        out_specs=VMEM,
+        compiler_params=params,
+        cost_estimate=cost,
+    )()
+    sent, tick = lax.optimization_barrier((start_rows, tick))
+    over = lax.ppermute(sent, "tm", across)
     x, near, far, send_hot = pl.pallas_call(
         first_kernel,
         out_shape=(state, near_shape, near_shape, hot_cross),
-        in_specs=[HBM] * 3,
+        in_specs=[VMEM] + [HBM] * 3,
         out_specs=(VMEM,) * 4,
         scratch_shapes=[
             pltpu.VMEM(cross_elem.shape, i32),
@@ -414,7 +463,7 @@
             dma((3,)),
         ],
         compiler_params=params,
-    )(start_rows, cross_elem, cross_face)
+    )(tick, start_rows, cross_elem, cross_face)
     even = lax.ppermute(near, "mesh", evens)
     odd = lax.ppermute(near, "mesh", odds)
     jac_rows = inner_jac.transpose(0, 2, 1, 3)
@@ -458,10 +507,10 @@
         passed = pl.pallas_call(
             functools.partial(relay_kernel, cap),
             out_shape=near_shape,
-            in_specs=[VMEM] * 3,
+            in_specs=[VMEM] * 4,
             out_specs=VMEM,
             compiler_params=params,
-        )(even, odd, far)
+        )(even, odd, near, far)
         over, _ = lax.optimization_barrier((over, passed))
         terms = pl.pallas_call(
             functools.partial(combine_kernel, times),
@@ -473,6 +522,24 @@
         )(x, over)
         passed = lax.ppermute(passed, "mesh", opposite)
         x, _ = lax.optimization_barrier((x, terms))
+        beside = pl.pallas_call(
+            mark_kernel,
+            out_shape=struct((8, 128)),
+            in_specs=[VMEM],
+            out_specs=VMEM,
+            compiler_params=params,
+            cost_estimate=cost,
+        )(x)
+        passed, _ = lax.optimization_barrier((passed, beside))
+        edge = pl.pallas_call(
+            functools.partial(forward_kernel, cap),
+            out_shape=near_shape,
+            in_specs=[VMEM] * 2,
+            out_specs=VMEM,
+            compiler_params=params,
+        )(near, passed)
+        x, edge = lax.optimization_barrier((x, edge))
+        edge = lax.ppermute(edge, "mesh", edges)
         if sweep > 0:
             inner = pl.pallas_call(
                 inner_kernel,
@@ -500,12 +567,12 @@
         terms = lax.all_to_all(
             terms, "tm", split_axis=0, concat_axis=0, tiled=True, axis_index_groups=halves
         )
-        operands = (inner, even, odd, passed, *tables, terms, inverse)
+        operands = (inner, even, odd, passed, edge, *tables, terms, inverse)
         if last:
             out = pl.pallas_call(
                 functools.partial(last_kernel, cap),
                 out_shape=struct((size, 1, elems)),
-                in_specs=[VMEM] * 11,
+                in_specs=[VMEM] * 12,
                 out_specs=HBM,
                 scratch_shapes=[
                     pltpu.VMEM((size, elems), f32),
@@ -518,7 +585,7 @@
         x, near, far = pl.pallas_call(
             functools.partial(middle_kernel, cap),
             out_shape=(state, near_shape, near_shape),
-            in_specs=[VMEM] * 12,
+            in_specs=[VMEM] * 13,
             out_specs=(VMEM,) * 3,
             scratch_shapes=[pltpu.VMEM((size, elems), f32)],
             compiler_params=params,

time: 87 us -> 83 us (0.954)
  waiting for transfers between devices: 16.8 us -> 12.6 us
  starting transfers between devices: 52.6 us -> 54.5 us
  local copies, waits for them, and re-layouts: 6.98 us -> 5.59 us
    ppermute x2, starting transfers between devices: 14.7 us -> 1.33 us  [on_device(): odd = lax.ppermute(near, 'mesh', odds)]
    ppermute x2, waiting for transfers between devices: 9.48 us -> 0.01 us  [on_device(): odd = lax.ppermute(near, 'mesh', odds)]
    ppermute x1 -> x3, starting transfers between devices: 15.7 us -> 24.6 us  [the longest x1 15.7 us: on_device(): over = lax.ppermute(sent, 'tm', across)]
    ppermute x1 -> x3, waiting for transfers between devices: 0.01 us -> 7.39 us  [the longest x2 7.39 us: on_device(): edge = lax.ppermute(edge, 'mesh', edges)]
    all_to_all x2, waiting for transfers between devices: 6.19 us -> 0.01 us  [on_device(): lax.all_to_all(terms, 'tm', split_axis=0, concat_axis=0, tiled=True, axis...]
    ppermute x2, starting transfers between devices: 3.84 us -> 6.68 us  [on_device(): even = lax.ppermute(near, 'mesh', evens)]
    ppermute x1, waiting for transfers between devices: 0.01 us -> 2.84 us  [on_device(): over = lax.ppermute(x, 'tm', across)]
    ppermute x1, starting transfers between devices: 3.93 us -> 6.19 us  [on_device(): over = lax.ppermute(x, 'tm', across)]
  transfers between devices with their start and end apart: 10 -> 12, of which waited for: 6 -> 6; matrix products, arithmetic and copies ran while one was open for 0% -> 0% of each run, Pallas kernels for 5% -> 6%
where the time goes in v3:
time: 83 us; the launch traced here: 82.4 us
  starting transfers between devices  54.5 us (66%)
  waiting for transfers between devices  12.6 us (15%)
  Pallas kernels  9.38 us (11%)
  local copies, waits for them, and re-layouts  5.59 us (7%)
    ppermute x1, starting transfers between devices, on_device(): over = lax.ppermute(sent, 'tm', across)  15.7 us
    all_to_all x2, starting transfers between devices, on_device(): lax.all_to_all(terms, 'tm', split_axis=0, concat_axis=0, tiled=True, axis...  9.48 us
    ppermute x2, starting transfers between devices, on_device(): edge = lax.ppermute(edge, 'mesh', edges)  8.86 us
    ppermute x2, waiting for transfers between devices, on_device(): edge = lax.ppermute(edge, 'mesh', edges)  7.39 us
    ppermute x2, starting transfers between devices, on_device(): even = lax.ppermute(near, 'mesh', evens)  6.68 us
    ppermute x2, starting transfers between devices, on_device(): passed = lax.ppermute(passed, 'mesh', opposite)  6.21 us
    ppermute x1, starting transfers between devices, on_device(): over = lax.ppermute(x, 'tm', across)  6.19 us
    unnamed x28, local copies, waits for them, and re-layouts  5.59 us
  transfers between devices with their start and end apart: 12, of which 6 were waited for; matrix products, arithmetic and copies ran while one was open for 0% of the time, Pallas kernels for 6%

profile of v3, /device:TPU:24, one launch (start us, length us, event | category | flops | bytes accessed | tf_op | source)
XLA Modules:
  0.0 82.4 jit_solution(3892693895078798192)
XLA Ops:
  0.0 0.9 %copy-done.2 = f32[1,135,128]{2,0,1:T(1,128)S(1)} copy-done((f32[1,135,128]{2,0,1:T(1,128)S(1)}, f32[1,135,128]{2,0,1:T(1,128)}, u32[]{:S(2)}) %copy-start.2) | copy-done | bytes 69144
  0.9 15.7 %collective-permute-start = (f32[135,1,128]{2,1,0:T(1,128)S(1)}, f32[135,1,128]{2,1,0:T(1,128)S(1)}, u32[]{:S(2)}, u32[]{:S(2)}) collective-permute-start(f32[135,1,128]{2,1,0:T(1,128)S(1)} %bitcast.6), channel_id=1, source_target_pairs={{0,256},{64,320},{128,384},{192,448},{256,0},{320,64},{384,128},{4... | collective-permute-start | bytes 207368 | tf_op jit(solution)/shard_map/ppermute | solution.py:454
  17.9 4.8 %collective-permute-start.1 = (f32[72,128]{1,0:T(8,128)S(1)}, f32[72,128]{1,0:T(8,128)S(1)}, u32[]{:S(2)}, u32[]{:S(2)}) collective-permute-start(f32[72,128]{1,0:T(8,128)S(1)} %get-tuple-element.34.near_ref), channel_id=1, source_target_pairs={{0,1},{1,0},{2,3},{3,2},{4,5},{5,4},{6,7},{7,6},{8,9},{9,8},{10,11... | collective-permute-start | bytes 110600 | tf_op jit(solution)/shard_map/ppermute | solution.py:467
  22.6 0.8 %collective-permute-done.1.even_ref.refs_1_ = f32[72,128]{1,0:T(8,128)S(1)} collective-permute-done((f32[72,128]{1,0:T(8,128)S(1)}, f32[72,128]{1,0:T(8,128)S(1)}, u32[]{:S(2)}, u32[]{:S(2)}) %collective-permute-start.1) | collective-permute-done | bytes 36896 | tf_op jit(solution)/shard_map/ppermute | solution.py:467
  23.6 4.3 %collective-permute-start.3 = (f32[72,128]{1,0:T(8,128)S(1)}, f32[72,128]{1,0:T(8,128)S(1)}, u32[]{:S(2)}, u32[]{:S(2)}) collective-permute-start(f32[72,128]{1,0:T(8,128)S(1)} %shard_map.129), channel_id=1, source_target_pairs={{0,32},{1,33},{2,34},{3,35},{4,36},{5,37},{6,38},{7,39},{8,40},{9,... | collective-permute-start | bytes 110600 | tf_op jit(solution)/shard_map/ppermute | solution.py:523
  28.1 0.9 %shard_map.130 = f32[4,135,128]{2,1,0:T(8,128)} custom-call(f32[135,128]{1,0:T(8,128)S(1)} %get-tuple-element.38.x_ref, f32[135,1,128]{2,1,0:T(1,128)S(1)} %collective-permute-done.z_ref), custom_call_target="tpu_custom_call" | custom-call | flops 4000000000 | bytes 1000000 | tf_op jit(solution)/shard_map/pallas_call | solution.py:515
  29.0 4.7 %all-to-all-start = ((f32[4,135,128]{2,1,0:T(8,128)}), f32[4,135,128]{2,1,0:T(8,128)S(1)}, u32[]{:S(2)}, u32[]{:S(2)}) async-start(f32[4,135,128]{2,1,0:T(8,128)} %shard_map.130), calls=%async_computation | async-start | bytes 557056 | tf_op jit(solution)/shard_map/all_to_all | solution.py:567
  33.8 3.7 %collective-permute-start.4 = (f32[72,128]{1,0:T(8,128)S(1)}, f32[72,128]{1,0:T(8,128)S(1)}, u32[]{:S(2)}, u32[]{:S(2)}) collective-permute-start(f32[72,128]{1,0:T(8,128)S(1)} %shard_map.131), channel_id=1, source_target_pairs={{0,31},{31,0},{32,63},{63,32},{64,95},{95,64},{96,127},{127,96},{1... | collective-permute-start | bytes 110600 | tf_op jit(solution)/shard_map/ppermute | solution.py:542
  37.6 1.3 %shard_map.132 = (f32[216,128]{1,0:T(8,128)S(1)}, bf16[768,512]{1,0:T(8,128)(2,1)S(1)}, s32[1,512]{1,0:T(1,128)S(1)}, f32[40,512]{1,0:T(8,128)S(1)}, bf16[768,25...) custom-call(f32[135,128]{1,0:T(8,128)S(1)} %get-tuple-element.38.x_r, ...), custom_call_target="tpu_custom_call" | custom-call | flops 4000000000 | bytes 1000000 | tf_op jit(solution)/shard_map/pallas_call | solution.py:553
  38.9 4.1 %collective-permute-done.4.refs_4_ = f32[72,128]{1,0:T(8,128)S(1)} collective-permute-done((f32[72,128]{1,0:T(8,128)S(1)}, f32[72,128]{1,0:T(8,128)S(1)}, u32[]{:S(2)}, u32[]{:S(2)}) %collective-permute-start.4) | collective-permute-done | bytes 36896 | tf_op jit(solution)/shard_map/ppermute | solution.py:542
  43.0 2.3 %copy-done = bf16[1,135,135,128]{3,2,1,0:T(8,128)(2,1)S(1)} copy-done((bf16[1,135,135,128]{3,2,1,0:T(8,128)(2,1)S(1)}, bf16[1,135,135,128]{3,2,1,0:T(8,128)(2,1)}, u32[]{:S(2)}) %copy-start) | copy-done | bytes 4665624
  45.3 2.1 %shard_map.133 = (f32[135,128]{1,0:T(8,128)S(1)}, f32[72,128]{1,0:T(8,128)S(1)}, f32[72,128]{1,0:T(8,128)S(1)}) custom-call(f32[216,128]{1,0:T(8,128)S(1)} %get-tuple-element.39.refs_0_, f32[72,128]{1,0:T(8,128)S(1)} %collective-permute-done.1.even_ref.refs_1_, f32[72,128]{1,0:T(8,128)S(1)} %collective-permute-done.2.odd_ref.refs_2_, ...), custom_call_target="tpu_custom_call" | custom-call | tf_op jit(solution)/shard_map/pallas_call | solution.py:585
  47.5 6.2 %collective-permute-start.5 = (f32[135,128]{1,0:T(8,128)S(1)}, f32[135,128]{1,0:T(8,128)S(1)}, u32[]{:S(2)}, u32[]{:S(2)}) collective-permute-start(f32[135,128]{1,0:T(8,128)S(1)} %get-tuple-element.52.x_ref), channel_id=1, source_target_pairs={{0,256},{64,320},{128,384},{192,448},{256,0},{320,64},{384,128},{4... | collective-permute-start | bytes 207368 | tf_op jit(solution)/shard_map/ppermute | solution.py:504
  54.3 1.9 %collective-permute-start.6 = (f32[72,128]{1,0:T(8,128)S(1)}, f32[72,128]{1,0:T(8,128)S(1)}, u32[]{:S(2)}, u32[]{:S(2)}) collective-permute-start(f32[72,128]{1,0:T(8,128)S(1)} %get-tuple-element.48.near_ref), channel_id=1, source_target_pairs={{0,1},{1,0},{2,3},{3,2},{4,5},{5,4},{6,7},{7,6},{8,9},{9,8},{10,11... | collective-permute-start | bytes 110600 | tf_op jit(solution)/shard_map/ppermute | solution.py:505
  56.3 1.2 %collective-permute-done.6.even_ref.refs_1_ = f32[72,128]{1,0:T(8,128)S(1)} collective-permute-done((f32[72,128]{1,0:T(8,128)S(1)}, f32[72,128]{1,0:T(8,128)S(1)}, u32[]{:S(2)}, u32[]{:S(2)}) %collective-permute-start.6) | collective-permute-done | bytes 36896 | tf_op jit(solution)/shard_map/ppermute | solution.py:505
  57.6 1.9 %collective-permute-start.8 = (f32[72,128]{1,0:T(8,128)S(1)}, f32[72,128]{1,0:T(8,128)S(1)}, u32[]{:S(2)}, u32[]{:S(2)}) collective-permute-start(f32[72,128]{1,0:T(8,128)S(1)} %shard_map.134), channel_id=1, source_target_pairs={{0,32},{1,33},{2,34},{3,35},{4,36},{5,37},{6,38},{7,39},{8,40},{9,... | collective-permute-start | bytes 110600 | tf_op jit(solution)/shard_map/ppermute | solution.py:523
  59.5 2.8 %collective-permute-done.5.z_ref = f32[135,128]{1,0:T(8,128)S(1)} collective-permute-done((f32[135,128]{1,0:T(8,128)S(1)}, f32[135,128]{1,0:T(8,128)S(1)}, u32[]{:S(2)}, u32[]{:S(2)}) %collective-permute-start.5) | collective-permute-done | bytes 69152 | tf_op jit(solution)/shard_map/ppermute | solution.py:504
  62.4 0.7 shard_map.135
  63.1 4.8 %all-to-all-start.1 = ((f32[4,135,128]{2,1,0:T(8,128)}), f32[4,135,128]{2,1,0:T(8,128)S(1)}, u32[]{:S(2)}, u32[]{:S(2)}) async-start(f32[4,135,128]{2,1,0:T(8,128)} %shard_map.135), calls=%async_computation.1 | async-start | bytes 557056 | tf_op jit(solution)/shard_map/all_to_all | solution.py:567
  68.4 5.1 %collective-permute-start.9 = (f32[72,128]{1,0:T(8,128)S(1)}, f32[72,128]{1,0:T(8,128)S(1)}, u32[]{:S(2)}, u32[]{:S(2)}) collective-permute-start(f32[72,128]{1,0:T(8,128)S(1)} %shard_map.136), channel_id=1, source_target_pairs={{0,31},{31,0},{32,63},{63,32},{64,95},{95,64},{96,127},{127,96},{1... | collective-permute-start | bytes 110600 | tf_op jit(solution)/shard_map/ppermute | solution.py:542
  73.5 0.7 shard_map.137.refs_0_
  74.2 3.3 %collective-permute-done.9.refs_4_ = f32[72,128]{1,0:T(8,128)S(1)} collective-permute-done((f32[72,128]{1,0:T(8,128)S(1)}, f32[72,128]{1,0:T(8,128)S(1)}, u32[]{:S(2)}, u32[]{:S(2)}) %collective-permute-start.9) | collective-permute-done | bytes 36896 | tf_op jit(solution)/shard_map/ppermute | solution.py:542
  77.6 2.3 %copy-done.1 = bf16[1,135,135,128]{3,2,1,0:T(8,128)(2,1)S(1)} copy-done((bf16[1,135,135,128]{3,2,1,0:T(8,128)(2,1)S(1)}, bf16[1,135,135,128]{3,2,1,0:T(8,128)(2,1)}, u32[]{:S(2)}) %copy-start.1) | copy-done | bytes 4665624
  79.9 2.5 %shard_map.138 = f32[135,1,128]{2,1,0:T(1,128)} custom-call(f32[216,128]{1,0:T(8,128)S(1)} %shard_map.137.refs_0_, f32[72,128]{1,0:T(8,128)S(1)} %collective-permute-done.6.even_ref.refs_1_, f32[72,128]{1,0:T(8,128)S(1)} %collective-permute-done.7.odd_ref.refs_2_, f32[72,128]{1,0:T(8,128)S(1)} %collective-permute-done.8.far_ref.refs_3_, ...), custom_call_target="tpu_custom_call" | custom-call | tf_op jit(solution)/shard_map/pallas_call | solution.py:572
  (40 shorter events, 2.9 us)
Async XLA Ops:
  0.0 16.6 %copy-start.4 = (s32[1,160]{1,0:T(1,128)S(1)}, s32[1,160]{1,0:T(1,128)}, u32[]{:S(2)}) copy-start(s32[1,160]{1,0:T(1,128)} %cross_face_hbm.1) | copy-start | bytes 1924
  0.0 16.6 %copy-start.3 = (s32[1,160]{1,0:T(1,128)S(1)}, s32[1,160]{1,0:T(1,128)}, u32[]{:S(2)}) copy-start(s32[1,160]{1,0:T(1,128)} %cross_elem_hbm.1) | copy-start | bytes 1924
  0.9 27.1 %collective-permute-start = (f32[135,1,128]{2,1,0:T(1,128)S(1)}, f32[135,1,128]{2,1,0:T(1,128)S(1)}, u32[]{:S(2)}, u32[]{:S(2)}) collective-permute-start(f32[135,1,128]{2,1,0:T(1,128)S(1)} %bitcast.6), channel_id=1, source_target_pairs={{0,256},{64,320},{128,384},{192,448},{256,0},{320,64},{384,128},{4... | collective-permute-start | bytes 207368 | tf_op jit(solution)/shard_map/ppermute | solution.py:454
  17.2 5.4 %collective-permute-start.2 = (f32[72,128]{1,0:T(8,128)S(1)}, f32[72,128]{1,0:T(8,128)S(1)}, u32[]{:S(2)}, u32[]{:S(2)}) collective-permute-start(f32[72,128]{1,0:T(8,128)S(1)} %get-tuple-element.34.near_ref), channel_id=1, source_target_pairs={{1,2},{2,1},{3,4},{4,3},{5,6},{6,5},{7,8},{8,7},{9,10},{10,9},{11,... | collective-permute-start | bytes 110600 | tf_op jit(solution)/shard_map/ppermute | solution.py:468
  17.9 5.6 %collective-permute-start.1 = (f32[72,128]{1,0:T(8,128)S(1)}, f32[72,128]{1,0:T(8,128)S(1)}, u32[]{:S(2)}, u32[]{:S(2)}) collective-permute-start(f32[72,128]{1,0:T(8,128)S(1)} %get-tuple-element.34.near_ref), channel_id=1, source_target_pairs={{0,1},{1,0},{2,3},{3,2},{4,5},{5,4},{6,7},{7,6},{8,9},{9,8},{10,11... | collective-permute-start | bytes 110600 | tf_op jit(solution)/shard_map/ppermute | solution.py:467
  23.6 10.1 %collective-permute-start.3 = (f32[72,128]{1,0:T(8,128)S(1)}, f32[72,128]{1,0:T(8,128)S(1)}, u32[]{:S(2)}, u32[]{:S(2)}) collective-permute-start(f32[72,128]{1,0:T(8,128)S(1)} %shard_map.129), channel_id=1, source_target_pairs={{0,32},{1,33},{2,34},{3,35},{4,36},{5,37},{6,38},{7,39},{8,40},{9,... | collective-permute-start | bytes 110600 | tf_op jit(solution)/shard_map/ppermute | solution.py:523
  28.0 9.6 %copy-start.5 = (f32[135,128]{1,0:T(8,128)S(1)}, f32[135,128]{1,0:T(8,128)}, u32[]{:S(2)}) copy-start(f32[135,128]{1,0:T(8,128)} %mass_hbm.1) | copy-start | bytes 207364
  28.0 9.6 %copy-start.6 = (f32[1,135,128]{2,0,1:T(1,128)S(1)}, f32[1,135,128]{2,0,1:T(1,128)}, u32[]{:S(2)}) copy-start(f32[1,135,128]{2,0,1:T(1,128)} %param.15) | copy-start | bytes 207364
  28.0 9.6 %copy-start.7 = (f32[1,2,25,256]{3,1,2,0:T(2,128)S(1)}, f32[1,2,25,256]{3,1,2,0:T(2,128)}, u32[]{:S(2)}) copy-start(f32[1,2,25,256]{3,1,2,0:T(2,128)} %param.20) | copy-start | bytes 153604
  28.0 9.6 %copy-start.8 = (f32[1,25,1,160]{3,2,1,0:T(1,128)S(1)}, f32[1,25,1,160]{3,2,1,0:T(1,128)}, u32[]{:S(2)}) copy-start(f32[1,25,1,160]{3,2,1,0:T(1,128)} %param.25) | copy-start | bytes 48004
  28.0 9.6 %copy-start.9 = (s32[2,256]{1,0:T(2,128)S(1)}, s32[2,256]{1,0:T(2,128)}, u32[]{:S(2)}) copy-start(s32[2,256]{1,0:T(2,128)} %elem_hbm.3) | copy-start | bytes 6148
  28.0 9.6 %copy-start.10 = (s32[2,256]{1,0:T(2,128)S(1)}, s32[2,256]{1,0:T(2,128)}, u32[]{:S(2)}) copy-start(s32[2,256]{1,0:T(2,128)} %face_hbm.3) | copy-start | bytes 6148
  28.0 9.6 %copy-start.11 = (s32[256]{0:T(256)S(1)}, s32[256]{0:T(256)}, u32[]{:S(2)}) copy-start(s32[256]{0:T(256)} %param.19) | copy-start | bytes 3076
  28.0 9.6 %copy-start.12 = (s32[1,160]{1,0:T(1,128)S(1)}, s32[1,160]{1,0:T(1,128)}, u32[]{:S(2)}) copy-start(s32[1,160]{1,0:T(1,128)} %cross_orient_hbm.1) | copy-start | bytes 1924
  28.1 9.6 %copy-start.13 = (s32[1,5]{1,0:T(1,128)S(1)}, s32[1,5]{1,0:T(1,128)}, u32[]{:S(2)}) copy-start(s32[1,5]{1,0:T(1,128)} %count_hbm.1) | copy-start | bytes 64
  29.0 14.0 %all-to-all-start = ((f32[4,135,128]{2,1,0:T(8,128)}), f32[4,135,128]{2,1,0:T(8,128)S(1)}, u32[]{:S(2)}, u32[]{:S(2)}) async-start(f32[4,135,128]{2,1,0:T(8,128)} %shard_map.130), calls=%async_computation | async-start | bytes 557056 | tf_op jit(solution)/shard_map/all_to_all | solution.py:567
  33.8 9.2 %collective-permute-start.4 = (f32[72,128]{1,0:T(8,128)S(1)}, f32[72,128]{1,0:T(8,128)S(1)}, u32[]{:S(2)}, u32[]{:S(2)}) collective-permute-start(f32[72,128]{1,0:T(8,128)S(1)} %shard_map.131), channel_id=1, source_target_pairs={{0,31},{31,0},{32,63},{63,32},{64,95},{95,64},{96,127},{127,96},{1... | collective-permute-start | bytes 110600 | tf_op jit(solution)/shard_map/ppermute | solution.py:542
  43.0 2.3 %copy-start = (bf16[1,135,135,128]{3,2,1,0:T(8,128)(2,1)S(1)}, bf16[1,135,135,128]{3,2,1,0:T(8,128)(2,1)}, u32[]{:S(2)}) copy-start(bf16[1,135,135,128]{3,2,1,0:T(8,128)(2,1)} %refs_11_.3) | copy-start | bytes 13996804
  47.5 14.9 %collective-permute-start.5 = (f32[135,128]{1,0:T(8,128)S(1)}, f32[135,128]{1,0:T(8,128)S(1)}, u32[]{:S(2)}, u32[]{:S(2)}) collective-permute-start(f32[135,128]{1,0:T(8,128)S(1)} %get-tuple-element.52.x_ref), channel_id=1, source_target_pairs={{0,256},{64,320},{128,384},{192,448},{256,0},{320,64},{384,128},{4... | collective-permute-start | bytes 207368 | tf_op jit(solution)/shard_map/ppermute | solution.py:504
  53.7 2.6 %collective-permute-start.7 = (f32[72,128]{1,0:T(8,128)S(1)}, f32[72,128]{1,0:T(8,128)S(1)}, u32[]{:S(2)}, u32[]{:S(2)}) collective-permute-start(f32[72,128]{1,0:T(8,128)S(1)} %get-tuple-element.48.near_ref), channel_id=1, source_target_pairs={{1,2},{2,1},{3,4},{4,3},{5,6},{6,5},{7,8},{8,7},{9,10},{10,9},{11,... | collective-permute-start | bytes 110600 | tf_op jit(solution)/shard_map/ppermute | solution.py:506
  54.3 3.1 %collective-permute-start.6 = (f32[72,128]{1,0:T(8,128)S(1)}, f32[72,128]{1,0:T(8,128)S(1)}, u32[]{:S(2)}, u32[]{:S(2)}) collective-permute-start(f32[72,128]{1,0:T(8,128)S(1)} %get-tuple-element.48.near_ref), channel_id=1, source_target_pairs={{0,1},{1,0},{2,3},{3,2},{4,5},{5,4},{6,7},{7,6},{8,9},{9,8},{10,11... | collective-permute-start | bytes 110600 | tf_op jit(solution)/shard_map/ppermute | solution.py:505
  57.6 10.7 %collective-permute-start.8 = (f32[72,128]{1,0:T(8,128)S(1)}, f32[72,128]{1,0:T(8,128)S(1)}, u32[]{:S(2)}, u32[]{:S(2)}) collective-permute-start(f32[72,128]{1,0:T(8,128)S(1)} %shard_map.134), channel_id=1, source_target_pairs={{0,32},{1,33},{2,34},{3,35},{4,36},{5,37},{6,38},{7,39},{8,40},{9,... | collective-permute-start | bytes 110600 | tf_op jit(solution)/shard_map/ppermute | solution.py:523
  63.1 14.4 %all-to-all-start.1 = ((f32[4,135,128]{2,1,0:T(8,128)}), f32[4,135,128]{2,1,0:T(8,128)S(1)}, u32[]{:S(2)}, u32[]{:S(2)}) async-start(f32[4,135,128]{2,1,0:T(8,128)} %shard_map.135), calls=%async_computation.1 | async-start | bytes 557056 | tf_op jit(solution)/shard_map/all_to_all | solution.py:567
  68.4 9.2 %collective-permute-start.9 = (f32[72,128]{1,0:T(8,128)S(1)}, f32[72,128]{1,0:T(8,128)S(1)}, u32[]{:S(2)}, u32[]{:S(2)}) collective-permute-start(f32[72,128]{1,0:T(8,128)S(1)} %shard_map.136), channel_id=1, source_target_pairs={{0,31},{31,0},{32,63},{63,32},{64,95},{95,64},{96,127},{127,96},{1... | collective-permute-start | bytes 110600 | tf_op jit(solution)/shard_map/ppermute | solution.py:542
  (2 other events, 3.2 us)

commit v4 on v3

--- a/solution.py
+++ b/solution.py
@@ -370,16 +370,18 @@
     return resid.astype(jnp.bfloat16).astype(jnp.float32)
 
 
-def middle_kernel(cap, *refs):
-    *operands, held_ref, send_ref, out_ref, near_ref, far_ref, resid_ref = refs
-    resid = residual(cap, *operands, resid_ref)
-    solve(held_ref, resid, out_ref, 0, held_ref.shape[1])
+def residual_kernel(cap, *refs):
+    *operands, out_ref, sum_ref = refs
+    out_ref[...] = residual(cap, *operands, sum_ref)
+
+
+def middle_kernel(resid_ref, held_ref, send_ref, out_ref, near_ref, far_ref):
+    solve(held_ref, resid_ref[...], out_ref, 0, held_ref.shape[1])
     cross_trace(out_ref, send_ref[...], near_ref, far_ref)
 
 
-def last_kernel(cap, *refs):
-    *operands, held_ref, result_ref, resid_ref, out_ref, sems = refs
-    resid = residual(cap, *operands, resid_ref)
+def last_kernel(resid_ref, held_ref, result_ref, out_ref, sems):
+    resid = resid_ref[...]
     per = held_ref.shape[1] // 3
     copies = []
     for c in range(3):
@@ -567,29 +569,32 @@
         terms = lax.all_to_all(
             terms, "tm", split_axis=0, concat_axis=0, tiled=True, axis_index_groups=halves
         )
-        operands = (inner, even, odd, passed, edge, *tables, terms, inverse)
+        resid = pl.pallas_call(
+            functools.partial(residual_kernel, cap),
+            out_shape=state,
+            in_specs=[VMEM] * 11,
+            out_specs=VMEM,
+            scratch_shapes=[pltpu.VMEM((size, elems), f32)],
+            compiler_params=params,
+            cost_estimate=cost,
+        )(inner, even, odd, passed, edge, *tables, terms)
         if last:
             out = pl.pallas_call(
-                functools.partial(last_kernel, cap),
+                last_kernel,
                 out_shape=struct((size, 1, elems)),
-                in_specs=[VMEM] * 12,
+                in_specs=[VMEM] * 2,
                 out_specs=HBM,
-                scratch_shapes=[
-                    pltpu.VMEM((size, elems), f32),
-                    pltpu.VMEM((size, elems), f32),
-                    dma((3,)),
-                ],
+                scratch_shapes=[pltpu.VMEM((size, elems), f32), dma((3,))],
                 compiler_params=params,
-            )(*operands)
+            )(resid, inverse)
             return out.transpose(1, 0, 2)
         x, near, far = pl.pallas_call(
-            functools.partial(middle_kernel, cap),
+            middle_kernel,
             out_shape=(state, near_shape, near_shape),
-            in_specs=[VMEM] * 13,
+            in_specs=[VMEM] * 3,
             out_specs=(VMEM,) * 3,
-            scratch_shapes=[pltpu.VMEM((size, elems), f32)],
             compiler_params=params,
-        )(*operands, send_hot)
+        )(resid, inverse, send_hot)
 
 
 def solution(mesh):

time: 83 us -> 82.3 us (level)
    unnamed x28 -> x30, local copies, waits for them, and re-layouts: 5.59 us -> 4.97 us
    pallas_call x2 -> x4, Pallas kernels: 4.6 us -> 4.56 us  [the longest x1 2.02 us: on_device(): pl.pallas_call(last_kernel, out_shape=struct((size, 1, elems)), in_specs=...]
where the time goes in v4:
time: 82.3 us; the launch traced here: 81.7 us
  starting transfers between devices  54.5 us (66%)
  waiting for transfers between devices  12.6 us (15%)
  Pallas kernels  9.34 us (11%)
  local copies, waits for them, and re-layouts  4.97 us (6%)
    ppermute x1, starting transfers between devices, on_device(): over = lax.ppermute(sent, 'tm', across)  15.7 us
    all_to_all x2, starting transfers between devices, on_device(): lax.all_to_all(terms, 'tm', split_axis=0, concat_axis=0, tiled=True, axis...  9.48 us
    ppermute x2, starting transfers between devices, on_device(): edge = lax.ppermute(edge, 'mesh', edges)  8.86 us
    ppermute x2, waiting for transfers between devices, on_device(): edge = lax.ppermute(edge, 'mesh', edges)  7.36 us
    ppermute x2, starting transfers between devices, on_device(): even = lax.ppermute(near, 'mesh', evens)  6.68 us
    ppermute x2, starting transfers between devices, on_device(): passed = lax.ppermute(passed, 'mesh', opposite)  6.21 us
    ppermute x1, starting transfers between devices, on_device(): over = lax.ppermute(x, 'tm', across)  6.19 us
    unnamed x30, local copies, waits for them, and re-layouts  4.97 us
  transfers between devices with their start and end apart: 12, of which 6 were waited for; matrix products, arithmetic and copies ran while one was open for 0% of the time, Pallas kernels for 6%

profile of v4, /device:TPU:24, one launch (start us, length us, event | category | flops | bytes accessed | tf_op | source)
XLA Modules:
  0.0 81.7 jit_solution(12053175179839338555)
XLA Ops:
  0.0 0.9 %copy-done.1 = f32[1,135,128]{2,0,1:T(1,128)S(1)} copy-done((f32[1,135,128]{2,0,1:T(1,128)S(1)}, f32[1,135,128]{2,0,1:T(1,128)}, u32[]{:S(2)}) %copy-start.1) | copy-done | bytes 69144
  0.9 15.7 %collective-permute-start = (f32[135,1,128]{2,1,0:T(1,128)S(1)}, f32[135,1,128]{2,1,0:T(1,128)S(1)}, u32[]{:S(2)}, u32[]{:S(2)}) collective-permute-start(f32[135,1,128]{2,1,0:T(1,128)S(1)} %bitcast.8), channel_id=1, source_target_pairs={{0,256},{64,320},{128,384},{192,448},{256,0},{320,64},{384,128},{4... | collective-permute-start | bytes 207368 | tf_op jit(solution)/shard_map/ppermute | solution.py:456
  17.9 4.8 %collective-permute-start.1 = (f32[72,128]{1,0:T(8,128)S(1)}, f32[72,128]{1,0:T(8,128)S(1)}, u32[]{:S(2)}, u32[]{:S(2)}) collective-permute-start(f32[72,128]{1,0:T(8,128)S(1)} %get-tuple-element.34.near_ref), channel_id=1, source_target_pairs={{0,1},{1,0},{2,3},{3,2},{4,5},{5,4},{6,7},{7,6},{8,9},{9,8},{10,11... | collective-permute-start | bytes 110600 | tf_op jit(solution)/shard_map/ppermute | solution.py:469
  22.6 0.8 %collective-permute-done.1.even_ref.refs_1_ = f32[72,128]{1,0:T(8,128)S(1)} collective-permute-done((f32[72,128]{1,0:T(8,128)S(1)}, f32[72,128]{1,0:T(8,128)S(1)}, u32[]{:S(2)}, u32[]{:S(2)}) %collective-permute-start.1) | collective-permute-done | bytes 36896 | tf_op jit(solution)/shard_map/ppermute | solution.py:469
  23.6 4.3 %collective-permute-start.3 = (f32[72,128]{1,0:T(8,128)S(1)}, f32[72,128]{1,0:T(8,128)S(1)}, u32[]{:S(2)}, u32[]{:S(2)}) collective-permute-start(f32[72,128]{1,0:T(8,128)S(1)} %shard_map.129), channel_id=1, source_target_pairs={{0,32},{1,33},{2,34},{3,35},{4,36},{5,37},{6,38},{7,39},{8,40},{9,... | collective-permute-start | bytes 110600 | tf_op jit(solution)/shard_map/ppermute | solution.py:525
  28.1 0.9 %shard_map.130 = f32[4,135,128]{2,1,0:T(8,128)} custom-call(f32[135,128]{1,0:T(8,128)S(1)} %get-tuple-element.38.x_ref, f32[135,1,128]{2,1,0:T(1,128)S(1)} %collective-permute-done.z_ref), custom_call_target="tpu_custom_call" | custom-call | flops 4000000000 | bytes 1000000 | tf_op jit(solution)/shard_map/pallas_call | solution.py:517
  29.0 4.7 %all-to-all-start = ((f32[4,135,128]{2,1,0:T(8,128)}), f32[4,135,128]{2,1,0:T(8,128)S(1)}, u32[]{:S(2)}, u32[]{:S(2)}) async-start(f32[4,135,128]{2,1,0:T(8,128)} %shard_map.130), calls=%async_computation | async-start | bytes 557056 | tf_op jit(solution)/shard_map/all_to_all | solution.py:569
  33.8 3.7 %collective-permute-start.4 = (f32[72,128]{1,0:T(8,128)S(1)}, f32[72,128]{1,0:T(8,128)S(1)}, u32[]{:S(2)}, u32[]{:S(2)}) collective-permute-start(f32[72,128]{1,0:T(8,128)S(1)} %shard_map.131), channel_id=1, source_target_pairs={{0,31},{31,0},{32,63},{63,32},{64,95},{95,64},{96,127},{127,96},{1... | collective-permute-start | bytes 110600 | tf_op jit(solution)/shard_map/ppermute | solution.py:544
  37.6 1.3 %shard_map.132 = (f32[216,128]{1,0:T(8,128)S(1)}, bf16[768,512]{1,0:T(8,128)(2,1)S(1)}, s32[1,512]{1,0:T(1,128)S(1)}, f32[40,512]{1,0:T(8,128)S(1)}, bf16[768,25...) custom-call(f32[135,128]{1,0:T(8,128)S(1)} %get-tuple-element.38.x_r, ...), custom_call_target="tpu_custom_call" | custom-call | flops 4000000000 | bytes 1000000 | tf_op jit(solution)/shard_map/pallas_call | solution.py:555
  38.9 4.0 %collective-permute-done.4.refs_4_ = f32[72,128]{1,0:T(8,128)S(1)} collective-permute-done((f32[72,128]{1,0:T(8,128)S(1)}, f32[72,128]{1,0:T(8,128)S(1)}, u32[]{:S(2)}, u32[]{:S(2)}) %collective-permute-start.4) | collective-permute-done | bytes 36896 | tf_op jit(solution)/shard_map/ppermute | solution.py:544
  43.5 1.7 %slice-done.1 = s8[4194304]{0:T(1024)(128)(4,1)S(1)} async-done(((s8[4700160]{0:T(1024)(128)(4,1)}), s8[4194304]{0:T(1024)(128)(4,1)S(1)}, s32[]{:S(2)}) %slice-start.1) | async-done | bytes 4194328
  45.2 1.6 %shard_map.134 = (f32[135,128]{1,0:T(8,128)S(1)}, f32[72,128]{1,0:T(8,128)S(1)}, f32[72,128]{1,0:T(8,128)S(1)}) custom-call(f32[135,128]{1,0:T(8,128)S(1)} %shard_map.133.resid_ref, bf16[1,135,135,128]{3,2,1,0:T(8,128)(2,1)S(1)} %bitcast.7, bf16[768,256]{1,0:T(8,128)(2,1)S(1)} %get-tuple-element.46.send_ref), custom_call_target="tpu_custom_call" | custom-call | tf_op jit(solution)/shard_map/pallas_call | solution.py:591
  46.8 6.2 %collective-permute-start.5 = (f32[135,128]{1,0:T(8,128)S(1)}, f32[135,128]{1,0:T(8,128)S(1)}, u32[]{:S(2)}, u32[]{:S(2)}) collective-permute-start(f32[135,128]{1,0:T(8,128)S(1)} %get-tuple-element.52.x_ref), channel_id=1, source_target_pairs={{0,256},{64,320},{128,384},{192,448},{256,0},{320,64},{384,128},{4... | collective-permute-start | bytes 207368 | tf_op jit(solution)/shard_map/ppermute | solution.py:506
  53.7 1.9 %collective-permute-start.6 = (f32[72,128]{1,0:T(8,128)S(1)}, f32[72,128]{1,0:T(8,128)S(1)}, u32[]{:S(2)}, u32[]{:S(2)}) collective-permute-start(f32[72,128]{1,0:T(8,128)S(1)} %get-tuple-element.48.near_ref), channel_id=1, source_target_pairs={{0,1},{1,0},{2,3},{3,2},{4,5},{5,4},{6,7},{7,6},{8,9},{9,8},{10,11... | collective-permute-start | bytes 110600 | tf_op jit(solution)/shard_map/ppermute | solution.py:507
  55.6 1.2 %collective-permute-done.6.even_ref.refs_1_ = f32[72,128]{1,0:T(8,128)S(1)} collective-permute-done((f32[72,128]{1,0:T(8,128)S(1)}, f32[72,128]{1,0:T(8,128)S(1)}, u32[]{:S(2)}, u32[]{:S(2)}) %collective-permute-start.6) | collective-permute-done | bytes 36896 | tf_op jit(solution)/shard_map/ppermute | solution.py:507
  56.9 1.9 %collective-permute-start.8 = (f32[72,128]{1,0:T(8,128)S(1)}, f32[72,128]{1,0:T(8,128)S(1)}, u32[]{:S(2)}, u32[]{:S(2)}) collective-permute-start(f32[72,128]{1,0:T(8,128)S(1)} %shard_map.135), channel_id=1, source_target_pairs={{0,32},{1,33},{2,34},{3,35},{4,36},{5,37},{6,38},{7,39},{8,40},{9,... | collective-permute-start | bytes 110600 | tf_op jit(solution)/shard_map/ppermute | solution.py:525
  58.9 2.8 %collective-permute-done.5.z_ref = f32[135,128]{1,0:T(8,128)S(1)} collective-permute-done((f32[135,128]{1,0:T(8,128)S(1)}, f32[135,128]{1,0:T(8,128)S(1)}, u32[]{:S(2)}, u32[]{:S(2)}) %collective-permute-start.5) | collective-permute-done | bytes 69152 | tf_op jit(solution)/shard_map/ppermute | solution.py:506
  61.7 0.7 shard_map.136
  62.4 4.8 %all-to-all-start.1 = ((f32[4,135,128]{2,1,0:T(8,128)}), f32[4,135,128]{2,1,0:T(8,128)S(1)}, u32[]{:S(2)}, u32[]{:S(2)}) async-start(f32[4,135,128]{2,1,0:T(8,128)} %shard_map.136), calls=%async_computation.1 | async-start | bytes 557056 | tf_op jit(solution)/shard_map/all_to_all | solution.py:569
  67.7 5.2 %collective-permute-start.9 = (f32[72,128]{1,0:T(8,128)S(1)}, f32[72,128]{1,0:T(8,128)S(1)}, u32[]{:S(2)}, u32[]{:S(2)}) collective-permute-start(f32[72,128]{1,0:T(8,128)S(1)} %shard_map.137), channel_id=1, source_target_pairs={{0,31},{31,0},{32,63},{63,32},{64,95},{95,64},{96,127},{127,96},{1... | collective-permute-start | bytes 110600 | tf_op jit(solution)/shard_map/ppermute | solution.py:544
  72.9 0.7 shard_map.138.refs_0_
  73.6 3.3 %collective-permute-done.9.refs_4_ = f32[72,128]{1,0:T(8,128)S(1)} collective-permute-done((f32[72,128]{1,0:T(8,128)S(1)}, f32[72,128]{1,0:T(8,128)S(1)}, u32[]{:S(2)}, u32[]{:S(2)}) %collective-permute-start.9) | collective-permute-done | bytes 36896 | tf_op jit(solution)/shard_map/ppermute | solution.py:544
  77.4 2.3 %copy-done = bf16[1,135,135,128]{3,2,1,0:T(8,128)(2,1)S(1)} copy-done((bf16[1,135,135,128]{3,2,1,0:T(8,128)(2,1)S(1)}, bf16[1,135,135,128]{3,2,1,0:T(8,128)(2,1)}, u32[]{:S(2)}) %copy-start) | copy-done | bytes 4665624
  79.7 2.0 %shard_map.140 = f32[135,1,128]{2,1,0:T(1,128)} custom-call(f32[135,128]{1,0:T(8,128)S(1)} %shard_map.139.resid_ref, bf16[1,135,135,128]{3,2,1,0:T(8,128)(2,1)S(1)} %copy-done), custom_call_target="tpu_custom_call" | custom-call | tf_op jit(solution)/shard_map/pallas_call | solution.py:582
  (45 shorter events, 3.8 us)
Async XLA Ops:
  0.0 16.6 %copy-start.3 = (s32[1,160]{1,0:T(1,128)S(1)}, s32[1,160]{1,0:T(1,128)}, u32[]{:S(2)}) copy-start(s32[1,160]{1,0:T(1,128)} %cross_face_hbm.1) | copy-start | bytes 1924
  0.0 16.6 %copy-start.2 = (s32[1,160]{1,0:T(1,128)S(1)}, s32[1,160]{1,0:T(1,128)}, u32[]{:S(2)}) copy-start(s32[1,160]{1,0:T(1,128)} %cross_elem_hbm.1) | copy-start | bytes 1924
  0.9 27.1 %collective-permute-start = (f32[135,1,128]{2,1,0:T(1,128)S(1)}, f32[135,1,128]{2,1,0:T(1,128)S(1)}, u32[]{:S(2)}, u32[]{:S(2)}) collective-permute-start(f32[135,1,128]{2,1,0:T(1,128)S(1)} %bitcast.8), channel_id=1, source_target_pairs={{0,256},{64,320},{128,384},{192,448},{256,0},{320,64},{384,128},{4... | collective-permute-start | bytes 207368 | tf_op jit(solution)/shard_map/ppermute | solution.py:456
  17.2 5.4 %collective-permute-start.2 = (f32[72,128]{1,0:T(8,128)S(1)}, f32[72,128]{1,0:T(8,128)S(1)}, u32[]{:S(2)}, u32[]{:S(2)}) collective-permute-start(f32[72,128]{1,0:T(8,128)S(1)} %get-tuple-element.34.near_ref), channel_id=1, source_target_pairs={{1,2},{2,1},{3,4},{4,3},{5,6},{6,5},{7,8},{8,7},{9,10},{10,9},{11,... | collective-permute-start | bytes 110600 | tf_op jit(solution)/shard_map/ppermute | solution.py:470
  17.9 5.6 %collective-permute-start.1 = (f32[72,128]{1,0:T(8,128)S(1)}, f32[72,128]{1,0:T(8,128)S(1)}, u32[]{:S(2)}, u32[]{:S(2)}) collective-permute-start(f32[72,128]{1,0:T(8,128)S(1)} %get-tuple-element.34.near_ref), channel_id=1, source_target_pairs={{0,1},{1,0},{2,3},{3,2},{4,5},{5,4},{6,7},{7,6},{8,9},{9,8},{10,11... | collective-permute-start | bytes 110600 | tf_op jit(solution)/shard_map/ppermute | solution.py:469
  23.6 10.1 %collective-permute-start.3 = (f32[72,128]{1,0:T(8,128)S(1)}, f32[72,128]{1,0:T(8,128)S(1)}, u32[]{:S(2)}, u32[]{:S(2)}) collective-permute-start(f32[72,128]{1,0:T(8,128)S(1)} %shard_map.129), channel_id=1, source_target_pairs={{0,32},{1,33},{2,34},{3,35},{4,36},{5,37},{6,38},{7,39},{8,40},{9,... | collective-permute-start | bytes 110600 | tf_op jit(solution)/shard_map/ppermute | solution.py:525
  28.0 9.6 %copy-start.4 = (f32[135,128]{1,0:T(8,128)S(1)}, f32[135,128]{1,0:T(8,128)}, u32[]{:S(2)}) copy-start(f32[135,128]{1,0:T(8,128)} %mass_hbm.1) | copy-start | bytes 207364
  28.0 9.6 %copy-start.5 = (f32[1,135,128]{2,0,1:T(1,128)S(1)}, f32[1,135,128]{2,0,1:T(1,128)}, u32[]{:S(2)}) copy-start(f32[1,135,128]{2,0,1:T(1,128)} %param.15) | copy-start | bytes 207364
  28.0 9.6 %copy-start.6 = (f32[1,2,25,256]{3,1,2,0:T(2,128)S(1)}, f32[1,2,25,256]{3,1,2,0:T(2,128)}, u32[]{:S(2)}) copy-start(f32[1,2,25,256]{3,1,2,0:T(2,128)} %param.20) | copy-start | bytes 153604
  28.0 9.6 %copy-start.7 = (f32[1,25,1,160]{3,2,1,0:T(1,128)S(1)}, f32[1,25,1,160]{3,2,1,0:T(1,128)}, u32[]{:S(2)}) copy-start(f32[1,25,1,160]{3,2,1,0:T(1,128)} %param.25) | copy-start | bytes 48004
  28.0 9.6 %copy-start.8 = (s32[2,256]{1,0:T(2,128)S(1)}, s32[2,256]{1,0:T(2,128)}, u32[]{:S(2)}) copy-start(s32[2,256]{1,0:T(2,128)} %elem_hbm.3) | copy-start | bytes 6148
  28.0 9.6 %copy-start.9 = (s32[2,256]{1,0:T(2,128)S(1)}, s32[2,256]{1,0:T(2,128)}, u32[]{:S(2)}) copy-start(s32[2,256]{1,0:T(2,128)} %face_hbm.3) | copy-start | bytes 6148
  28.0 9.6 %copy-start.10 = (s32[256]{0:T(256)S(1)}, s32[256]{0:T(256)}, u32[]{:S(2)}) copy-start(s32[256]{0:T(256)} %param.19) | copy-start | bytes 3076
  28.0 9.6 %copy-start.11 = (s32[1,160]{1,0:T(1,128)S(1)}, s32[1,160]{1,0:T(1,128)}, u32[]{:S(2)}) copy-start(s32[1,160]{1,0:T(1,128)} %cross_orient_hbm.1) | copy-start | bytes 1924
  28.1 9.6 %copy-start.12 = (s32[1,5]{1,0:T(1,128)S(1)}, s32[1,5]{1,0:T(1,128)}, u32[]{:S(2)}) copy-start(s32[1,5]{1,0:T(1,128)} %count_hbm.1) | copy-start | bytes 64
  29.0 14.0 %all-to-all-start = ((f32[4,135,128]{2,1,0:T(8,128)}), f32[4,135,128]{2,1,0:T(8,128)S(1)}, u32[]{:S(2)}, u32[]{:S(2)}) async-start(f32[4,135,128]{2,1,0:T(8,128)} %shard_map.130), calls=%async_computation | async-start | bytes 557056 | tf_op jit(solution)/shard_map/all_to_all | solution.py:569
  33.8 9.2 %collective-permute-start.4 = (f32[72,128]{1,0:T(8,128)S(1)}, f32[72,128]{1,0:T(8,128)S(1)}, u32[]{:S(2)}, u32[]{:S(2)}) collective-permute-start(f32[72,128]{1,0:T(8,128)S(1)} %shard_map.131), channel_id=1, source_target_pairs={{0,31},{31,0},{32,63},{63,32},{64,95},{95,64},{96,127},{127,96},{1... | collective-permute-start | bytes 110600 | tf_op jit(solution)/shard_map/ppermute | solution.py:544
  37.6 5.9 %slice-start = ((s8[4700160]{0:T(1024)(128)(4,1)}), s8[505856]{0:T(1024)(128)(4,1)S(1)}, s32[]{:S(2)}) async-start(s8[4700160]{0:T(1024)(128)(4,1)} %bitcast.6), calls=%async_computation.2 | async-start | bytes 1011712
  46.8 14.9 %collective-permute-start.5 = (f32[135,128]{1,0:T(8,128)S(1)}, f32[135,128]{1,0:T(8,128)S(1)}, u32[]{:S(2)}, u32[]{:S(2)}) collective-permute-start(f32[135,128]{1,0:T(8,128)S(1)} %get-tuple-element.52.x_ref), channel_id=1, source_target_pairs={{0,256},{64,320},{128,384},{192,448},{256,0},{320,64},{384,128},{4... | collective-permute-start | bytes 207368 | tf_op jit(solution)/shard_map/ppermute | solution.py:506
  53.0 2.6 %collective-permute-start.7 = (f32[72,128]{1,0:T(8,128)S(1)}, f32[72,128]{1,0:T(8,128)S(1)}, u32[]{:S(2)}, u32[]{:S(2)}) collective-permute-start(f32[72,128]{1,0:T(8,128)S(1)} %get-tuple-element.48.near_ref), channel_id=1, source_target_pairs={{1,2},{2,1},{3,4},{4,3},{5,6},{6,5},{7,8},{8,7},{9,10},{10,9},{11,... | collective-permute-start | bytes 110600 | tf_op jit(solution)/shard_map/ppermute | solution.py:508
  53.7 3.1 %collective-permute-start.6 = (f32[72,128]{1,0:T(8,128)S(1)}, f32[72,128]{1,0:T(8,128)S(1)}, u32[]{:S(2)}, u32[]{:S(2)}) collective-permute-start(f32[72,128]{1,0:T(8,128)S(1)} %get-tuple-element.48.near_ref), channel_id=1, source_target_pairs={{0,1},{1,0},{2,3},{3,2},{4,5},{5,4},{6,7},{7,6},{8,9},{9,8},{10,11... | collective-permute-start | bytes 110600 | tf_op jit(solution)/shard_map/ppermute | solution.py:507
  56.9 10.7 %collective-permute-start.8 = (f32[72,128]{1,0:T(8,128)S(1)}, f32[72,128]{1,0:T(8,128)S(1)}, u32[]{:S(2)}, u32[]{:S(2)}) collective-permute-start(f32[72,128]{1,0:T(8,128)S(1)} %shard_map.135), channel_id=1, source_target_pairs={{0,32},{1,33},{2,34},{3,35},{4,36},{5,37},{6,38},{7,39},{8,40},{9,... | collective-permute-start | bytes 110600 | tf_op jit(solution)/shard_map/ppermute | solution.py:525
  62.4 14.4 %all-to-all-start.1 = ((f32[4,135,128]{2,1,0:T(8,128)}), f32[4,135,128]{2,1,0:T(8,128)S(1)}, u32[]{:S(2)}, u32[]{:S(2)}) async-start(f32[4,135,128]{2,1,0:T(8,128)} %shard_map.136), calls=%async_computation.1 | async-start | bytes 557056 | tf_op jit(solution)/shard_map/all_to_all | solution.py:569
  67.7 9.2 %collective-permute-start.9 = (f32[72,128]{1,0:T(8,128)S(1)}, f32[72,128]{1,0:T(8,128)S(1)}, u32[]{:S(2)}, u32[]{:S(2)}) collective-permute-start(f32[72,128]{1,0:T(8,128)S(1)} %shard_map.137), channel_id=1, source_target_pairs={{0,31},{31,0},{32,63},{63,32},{64,95},{95,64},{96,127},{127,96},{1... | collective-permute-start | bytes 110600 | tf_op jit(solution)/shard_map/ppermute | solution.py:544
  (3 other events, 5.4 us)

commit v5 on v4

--- a/solution.py
+++ b/solution.py
@@ -466,8 +466,8 @@
         ],
         compiler_params=params,
     )(tick, start_rows, cross_elem, cross_face)
+    odd = lax.ppermute(near, "mesh", odds)
     even = lax.ppermute(near, "mesh", evens)
-    odd = lax.ppermute(near, "mesh", odds)
     jac_rows = inner_jac.transpose(0, 2, 1, 3)
     cross_rows = cross_jac[0]
     prepare = pl.pallas_call(
@@ -504,8 +504,8 @@
         last = sweep == SWEEPS - 1
         if sweep > 0:
             over = lax.ppermute(x, "tm", across)
+            odd = lax.ppermute(near, "mesh", odds)
             even = lax.ppermute(near, "mesh", evens)
-            odd = lax.ppermute(near, "mesh", odds)
         passed = pl.pallas_call(
             functools.partial(relay_kernel, cap),
             out_shape=near_shape,

time: 82.3 us -> 82.3 us (level)
  no operation moved by 1% of the time
where the time goes in v5:
time: 82.3 us; the launch traced here: 81.7 us
  starting transfers between devices  54.5 us (66%)
  waiting for transfers between devices  12.6 us (15%)
  Pallas kernels  9.34 us (11%)
  local copies, waits for them, and re-layouts  4.97 us (6%)
    ppermute x1, starting transfers between devices, on_device(): over = lax.ppermute(sent, 'tm', across)  15.7 us
    all_to_all x2, starting transfers between devices, on_device(): lax.all_to_all(terms, 'tm', split_axis=0, concat_axis=0, tiled=True, axis...  9.48 us
    ppermute x2, starting transfers between devices, on_device(): edge = lax.ppermute(edge, 'mesh', edges)  8.86 us
    ppermute x2, waiting for transfers between devices, on_device(): edge = lax.ppermute(edge, 'mesh', edges)  7.36 us
    ppermute x2, starting transfers between devices, on_device(): even = lax.ppermute(near, 'mesh', evens)  6.68 us
    ppermute x2, starting transfers between devices, on_device(): passed = lax.ppermute(passed, 'mesh', opposite)  6.21 us
    ppermute x1, starting transfers between devices, on_device(): over = lax.ppermute(x, 'tm', across)  6.19 us
    unnamed x30, local copies, waits for them, and re-layouts  4.97 us
  transfers between devices with their start and end apart: 12, of which 6 were waited for; matrix products, arithmetic and copies ran while one was open for 0% of the time, Pallas kernels for 6%

profile of v5, /device:TPU:24, one launch (start us, length us, event | category | flops | bytes accessed | tf_op | source)
XLA Modules:
  0.0 81.7 jit_solution(12053175179839338555)
XLA Ops:
  0.0 0.9 %copy-done.1 = f32[1,135,128]{2,0,1:T(1,128)S(1)} copy-done((f32[1,135,128]{2,0,1:T(1,128)S(1)}, f32[1,135,128]{2,0,1:T(1,128)}, u32[]{:S(2)}) %copy-start.1) | copy-done | bytes 69144
  0.9 15.7 %collective-permute-start = (f32[135,1,128]{2,1,0:T(1,128)S(1)}, f32[135,1,128]{2,1,0:T(1,128)S(1)}, u32[]{:S(2)}, u32[]{:S(2)}) collective-permute-start(f32[135,1,128]{2,1,0:T(1,128)S(1)} %bitcast.8), channel_id=1, source_target_pairs={{0,256},{64,320},{128,384},{192,448},{256,0},{320,64},{384,128},{4... | collective-permute-start | bytes 207368 | tf_op jit(solution)/shard_map/ppermute | solution.py:456
  17.9 4.8 %collective-permute-start.1 = (f32[72,128]{1,0:T(8,128)S(1)}, f32[72,128]{1,0:T(8,128)S(1)}, u32[]{:S(2)}, u32[]{:S(2)}) collective-permute-start(f32[72,128]{1,0:T(8,128)S(1)} %get-tuple-element.34.near_ref), channel_id=1, source_target_pairs={{0,1},{1,0},{2,3},{3,2},{4,5},{5,4},{6,7},{7,6},{8,9},{9,8},{10,11... | collective-permute-start | bytes 110600 | tf_op jit(solution)/shard_map/ppermute | solution.py:470
  22.6 0.8 %collective-permute-done.1.even_ref.refs_1_ = f32[72,128]{1,0:T(8,128)S(1)} collective-permute-done((f32[72,128]{1,0:T(8,128)S(1)}, f32[72,128]{1,0:T(8,128)S(1)}, u32[]{:S(2)}, u32[]{:S(2)}) %collective-permute-start.1) | collective-permute-done | bytes 36896 | tf_op jit(solution)/shard_map/ppermute | solution.py:470
  23.6 4.3 %collective-permute-start.3 = (f32[72,128]{1,0:T(8,128)S(1)}, f32[72,128]{1,0:T(8,128)S(1)}, u32[]{:S(2)}, u32[]{:S(2)}) collective-permute-start(f32[72,128]{1,0:T(8,128)S(1)} %shard_map.129), channel_id=1, source_target_pairs={{0,32},{1,33},{2,34},{3,35},{4,36},{5,37},{6,38},{7,39},{8,40},{9,... | collective-permute-start | bytes 110600 | tf_op jit(solution)/shard_map/ppermute | solution.py:525
  28.1 0.9 %shard_map.130 = f32[4,135,128]{2,1,0:T(8,128)} custom-call(f32[135,128]{1,0:T(8,128)S(1)} %get-tuple-element.38.x_ref, f32[135,1,128]{2,1,0:T(1,128)S(1)} %collective-permute-done.z_ref), custom_call_target="tpu_custom_call" | custom-call | flops 4000000000 | bytes 1000000 | tf_op jit(solution)/shard_map/pallas_call | solution.py:517
  29.0 4.7 %all-to-all-start = ((f32[4,135,128]{2,1,0:T(8,128)}), f32[4,135,128]{2,1,0:T(8,128)S(1)}, u32[]{:S(2)}, u32[]{:S(2)}) async-start(f32[4,135,128]{2,1,0:T(8,128)} %shard_map.130), calls=%async_computation | async-start | bytes 557056 | tf_op jit(solution)/shard_map/all_to_all | solution.py:569
  33.8 3.7 %collective-permute-start.4 = (f32[72,128]{1,0:T(8,128)S(1)}, f32[72,128]{1,0:T(8,128)S(1)}, u32[]{:S(2)}, u32[]{:S(2)}) collective-permute-start(f32[72,128]{1,0:T(8,128)S(1)} %shard_map.131), channel_id=1, source_target_pairs={{0,31},{31,0},{32,63},{63,32},{64,95},{95,64},{96,127},{127,96},{1... | collective-permute-start | bytes 110600 | tf_op jit(solution)/shard_map/ppermute | solution.py:544
  37.6 1.3 %shard_map.132 = (f32[216,128]{1,0:T(8,128)S(1)}, bf16[768,512]{1,0:T(8,128)(2,1)S(1)}, s32[1,512]{1,0:T(1,128)S(1)}, f32[40,512]{1,0:T(8,128)S(1)}, bf16[768,25...) custom-call(f32[135,128]{1,0:T(8,128)S(1)} %get-tuple-element.38.x_r, ...), custom_call_target="tpu_custom_call" | custom-call | flops 4000000000 | bytes 1000000 | tf_op jit(solution)/shard_map/pallas_call | solution.py:555
  38.9 4.0 %collective-permute-done.4.refs_4_ = f32[72,128]{1,0:T(8,128)S(1)} collective-permute-done((f32[72,128]{1,0:T(8,128)S(1)}, f32[72,128]{1,0:T(8,128)S(1)}, u32[]{:S(2)}, u32[]{:S(2)}) %collective-permute-start.4) | collective-permute-done | bytes 36896 | tf_op jit(solution)/shard_map/ppermute | solution.py:544
  43.5 1.7 %slice-done.1 = s8[4194304]{0:T(1024)(128)(4,1)S(1)} async-done(((s8[4700160]{0:T(1024)(128)(4,1)}), s8[4194304]{0:T(1024)(128)(4,1)S(1)}, s32[]{:S(2)}) %slice-start.1) | async-done | bytes 4194328
  45.2 1.6 %shard_map.134 = (f32[135,128]{1,0:T(8,128)S(1)}, f32[72,128]{1,0:T(8,128)S(1)}, f32[72,128]{1,0:T(8,128)S(1)}) custom-call(f32[135,128]{1,0:T(8,128)S(1)} %shard_map.133.resid_ref, bf16[1,135,135,128]{3,2,1,0:T(8,128)(2,1)S(1)} %bitcast.7, bf16[768,256]{1,0:T(8,128)(2,1)S(1)} %get-tuple-element.46.send_ref), custom_call_target="tpu_custom_call" | custom-call | tf_op jit(solution)/shard_map/pallas_call | solution.py:591
  46.8 6.2 %collective-permute-start.5 = (f32[135,128]{1,0:T(8,128)S(1)}, f32[135,128]{1,0:T(8,128)S(1)}, u32[]{:S(2)}, u32[]{:S(2)}) collective-permute-start(f32[135,128]{1,0:T(8,128)S(1)} %get-tuple-element.52.x_ref), channel_id=1, source_target_pairs={{0,256},{64,320},{128,384},{192,448},{256,0},{320,64},{384,128},{4... | collective-permute-start | bytes 207368 | tf_op jit(solution)/shard_map/ppermute | solution.py:506
  53.7 1.9 %collective-permute-start.6 = (f32[72,128]{1,0:T(8,128)S(1)}, f32[72,128]{1,0:T(8,128)S(1)}, u32[]{:S(2)}, u32[]{:S(2)}) collective-permute-start(f32[72,128]{1,0:T(8,128)S(1)} %get-tuple-element.48.near_ref), channel_id=1, source_target_pairs={{0,1},{1,0},{2,3},{3,2},{4,5},{5,4},{6,7},{7,6},{8,9},{9,8},{10,11... | collective-permute-start | bytes 110600 | tf_op jit(solution)/shard_map/ppermute | solution.py:508
  55.6 1.2 %collective-permute-done.6.even_ref.refs_1_ = f32[72,128]{1,0:T(8,128)S(1)} collective-permute-done((f32[72,128]{1,0:T(8,128)S(1)}, f32[72,128]{1,0:T(8,128)S(1)}, u32[]{:S(2)}, u32[]{:S(2)}) %collective-permute-start.6) | collective-permute-done | bytes 36896 | tf_op jit(solution)/shard_map/ppermute | solution.py:508
  56.9 1.9 %collective-permute-start.8 = (f32[72,128]{1,0:T(8,128)S(1)}, f32[72,128]{1,0:T(8,128)S(1)}, u32[]{:S(2)}, u32[]{:S(2)}) collective-permute-start(f32[72,128]{1,0:T(8,128)S(1)} %shard_map.135), channel_id=1, source_target_pairs={{0,32},{1,33},{2,34},{3,35},{4,36},{5,37},{6,38},{7,39},{8,40},{9,... | collective-permute-start | bytes 110600 | tf_op jit(solution)/shard_map/ppermute | solution.py:525
  58.9 2.8 %collective-permute-done.5.z_ref = f32[135,128]{1,0:T(8,128)S(1)} collective-permute-done((f32[135,128]{1,0:T(8,128)S(1)}, f32[135,128]{1,0:T(8,128)S(1)}, u32[]{:S(2)}, u32[]{:S(2)}) %collective-permute-start.5) | collective-permute-done | bytes 69152 | tf_op jit(solution)/shard_map/ppermute | solution.py:506
  61.7 0.7 shard_map.136
  62.4 4.8 %all-to-all-start.1 = ((f32[4,135,128]{2,1,0:T(8,128)}), f32[4,135,128]{2,1,0:T(8,128)S(1)}, u32[]{:S(2)}, u32[]{:S(2)}) async-start(f32[4,135,128]{2,1,0:T(8,128)} %shard_map.136), calls=%async_computation.1 | async-start | bytes 557056 | tf_op jit(solution)/shard_map/all_to_all | solution.py:569
  67.7 5.2 %collective-permute-start.9 = (f32[72,128]{1,0:T(8,128)S(1)}, f32[72,128]{1,0:T(8,128)S(1)}, u32[]{:S(2)}, u32[]{:S(2)}) collective-permute-start(f32[72,128]{1,0:T(8,128)S(1)} %shard_map.137), channel_id=1, source_target_pairs={{0,31},{31,0},{32,63},{63,32},{64,95},{95,64},{96,127},{127,96},{1... | collective-permute-start | bytes 110600 | tf_op jit(solution)/shard_map/ppermute | solution.py:544
  72.9 0.7 shard_map.138.refs_0_
  73.6 3.3 %collective-permute-done.9.refs_4_ = f32[72,128]{1,0:T(8,128)S(1)} collective-permute-done((f32[72,128]{1,0:T(8,128)S(1)}, f32[72,128]{1,0:T(8,128)S(1)}, u32[]{:S(2)}, u32[]{:S(2)}) %collective-permute-start.9) | collective-permute-done | bytes 36896 | tf_op jit(solution)/shard_map/ppermute | solution.py:544
  77.4 2.3 %copy-done = bf16[1,135,135,128]{3,2,1,0:T(8,128)(2,1)S(1)} copy-done((bf16[1,135,135,128]{3,2,1,0:T(8,128)(2,1)S(1)}, bf16[1,135,135,128]{3,2,1,0:T(8,128)(2,1)}, u32[]{:S(2)}) %copy-start) | copy-done | bytes 4665624
  79.7 2.0 %shard_map.140 = f32[135,1,128]{2,1,0:T(1,128)} custom-call(f32[135,128]{1,0:T(8,128)S(1)} %shard_map.139.resid_ref, bf16[1,135,135,128]{3,2,1,0:T(8,128)(2,1)S(1)} %copy-done), custom_call_target="tpu_custom_call" | custom-call | tf_op jit(solution)/shard_map/pallas_call | solution.py:582
  (45 shorter events, 3.8 us)
Async XLA Ops:
  0.0 16.6 %copy-start.3 = (s32[1,160]{1,0:T(1,128)S(1)}, s32[1,160]{1,0:T(1,128)}, u32[]{:S(2)}) copy-start(s32[1,160]{1,0:T(1,128)} %cross_face_hbm.1) | copy-start | bytes 1924
  0.0 16.6 %copy-start.2 = (s32[1,160]{1,0:T(1,128)S(1)}, s32[1,160]{1,0:T(1,128)}, u32[]{:S(2)}) copy-start(s32[1,160]{1,0:T(1,128)} %cross_elem_hbm.1) | copy-start | bytes 1924
  0.9 27.1 %collective-permute-start = (f32[135,1,128]{2,1,0:T(1,128)S(1)}, f32[135,1,128]{2,1,0:T(1,128)S(1)}, u32[]{:S(2)}, u32[]{:S(2)}) collective-permute-start(f32[135,1,128]{2,1,0:T(1,128)S(1)} %bitcast.8), channel_id=1, source_target_pairs={{0,256},{64,320},{128,384},{192,448},{256,0},{320,64},{384,128},{4... | collective-permute-start | bytes 207368 | tf_op jit(solution)/shard_map/ppermute | solution.py:456
  17.2 5.4 %collective-permute-start.2 = (f32[72,128]{1,0:T(8,128)S(1)}, f32[72,128]{1,0:T(8,128)S(1)}, u32[]{:S(2)}, u32[]{:S(2)}) collective-permute-start(f32[72,128]{1,0:T(8,128)S(1)} %get-tuple-element.34.near_ref), channel_id=1, source_target_pairs={{1,2},{2,1},{3,4},{4,3},{5,6},{6,5},{7,8},{8,7},{9,10},{10,9},{11,... | collective-permute-start | bytes 110600 | tf_op jit(solution)/shard_map/ppermute | solution.py:469
  17.9 5.6 %collective-permute-start.1 = (f32[72,128]{1,0:T(8,128)S(1)}, f32[72,128]{1,0:T(8,128)S(1)}, u32[]{:S(2)}, u32[]{:S(2)}) collective-permute-start(f32[72,128]{1,0:T(8,128)S(1)} %get-tuple-element.34.near_ref), channel_id=1, source_target_pairs={{0,1},{1,0},{2,3},{3,2},{4,5},{5,4},{6,7},{7,6},{8,9},{9,8},{10,11... | collective-permute-start | bytes 110600 | tf_op jit(solution)/shard_map/ppermute | solution.py:470
  23.6 10.1 %collective-permute-start.3 = (f32[72,128]{1,0:T(8,128)S(1)}, f32[72,128]{1,0:T(8,128)S(1)}, u32[]{:S(2)}, u32[]{:S(2)}) collective-permute-start(f32[72,128]{1,0:T(8,128)S(1)} %shard_map.129), channel_id=1, source_target_pairs={{0,32},{1,33},{2,34},{3,35},{4,36},{5,37},{6,38},{7,39},{8,40},{9,... | collective-permute-start | bytes 110600 | tf_op jit(solution)/shard_map/ppermute | solution.py:525
  28.0 9.6 %copy-start.4 = (f32[135,128]{1,0:T(8,128)S(1)}, f32[135,128]{1,0:T(8,128)}, u32[]{:S(2)}) copy-start(f32[135,128]{1,0:T(8,128)} %mass_hbm.1) | copy-start | bytes 207364
  28.0 9.6 %copy-start.5 = (f32[1,135,128]{2,0,1:T(1,128)S(1)}, f32[1,135,128]{2,0,1:T(1,128)}, u32[]{:S(2)}) copy-start(f32[1,135,128]{2,0,1:T(1,128)} %param.15) | copy-start | bytes 207364
  28.0 9.6 %copy-start.6 = (f32[1,2,25,256]{3,1,2,0:T(2,128)S(1)}, f32[1,2,25,256]{3,1,2,0:T(2,128)}, u32[]{:S(2)}) copy-start(f32[1,2,25,256]{3,1,2,0:T(2,128)} %param.20) | copy-start | bytes 153604
  28.0 9.6 %copy-start.7 = (f32[1,25,1,160]{3,2,1,0:T(1,128)S(1)}, f32[1,25,1,160]{3,2,1,0:T(1,128)}, u32[]{:S(2)}) copy-start(f32[1,25,1,160]{3,2,1,0:T(1,128)} %param.25) | copy-start | bytes 48004
  28.0 9.6 %copy-start.8 = (s32[2,256]{1,0:T(2,128)S(1)}, s32[2,256]{1,0:T(2,128)}, u32[]{:S(2)}) copy-start(s32[2,256]{1,0:T(2,128)} %elem_hbm.3) | copy-start | bytes 6148
  28.0 9.6 %copy-start.9 = (s32[2,256]{1,0:T(2,128)S(1)}, s32[2,256]{1,0:T(2,128)}, u32[]{:S(2)}) copy-start(s32[2,256]{1,0:T(2,128)} %face_hbm.3) | copy-start | bytes 6148
  28.0 9.6 %copy-start.10 = (s32[256]{0:T(256)S(1)}, s32[256]{0:T(256)}, u32[]{:S(2)}) copy-start(s32[256]{0:T(256)} %param.19) | copy-start | bytes 3076
  28.0 9.6 %copy-start.11 = (s32[1,160]{1,0:T(1,128)S(1)}, s32[1,160]{1,0:T(1,128)}, u32[]{:S(2)}) copy-start(s32[1,160]{1,0:T(1,128)} %cross_orient_hbm.1) | copy-start | bytes 1924
  28.1 9.6 %copy-start.12 = (s32[1,5]{1,0:T(1,128)S(1)}, s32[1,5]{1,0:T(1,128)}, u32[]{:S(2)}) copy-start(s32[1,5]{1,0:T(1,128)} %count_hbm.1) | copy-start | bytes 64
  29.0 14.0 %all-to-all-start = ((f32[4,135,128]{2,1,0:T(8,128)}), f32[4,135,128]{2,1,0:T(8,128)S(1)}, u32[]{:S(2)}, u32[]{:S(2)}) async-start(f32[4,135,128]{2,1,0:T(8,128)} %shard_map.130), calls=%async_computation | async-start | bytes 557056 | tf_op jit(solution)/shard_map/all_to_all | solution.py:569
  33.8 9.2 %collective-permute-start.4 = (f32[72,128]{1,0:T(8,128)S(1)}, f32[72,128]{1,0:T(8,128)S(1)}, u32[]{:S(2)}, u32[]{:S(2)}) collective-permute-start(f32[72,128]{1,0:T(8,128)S(1)} %shard_map.131), channel_id=1, source_target_pairs={{0,31},{31,0},{32,63},{63,32},{64,95},{95,64},{96,127},{127,96},{1... | collective-permute-start | bytes 110600 | tf_op jit(solution)/shard_map/ppermute | solution.py:544
  37.6 5.9 %slice-start = ((s8[4700160]{0:T(1024)(128)(4,1)}), s8[505856]{0:T(1024)(128)(4,1)S(1)}, s32[]{:S(2)}) async-start(s8[4700160]{0:T(1024)(128)(4,1)} %bitcast.6), calls=%async_computation.2 | async-start | bytes 1011712
  46.8 14.9 %collective-permute-start.5 = (f32[135,128]{1,0:T(8,128)S(1)}, f32[135,128]{1,0:T(8,128)S(1)}, u32[]{:S(2)}, u32[]{:S(2)}) collective-permute-start(f32[135,128]{1,0:T(8,128)S(1)} %get-tuple-element.52.x_ref), channel_id=1, source_target_pairs={{0,256},{64,320},{128,384},{192,448},{256,0},{320,64},{384,128},{4... | collective-permute-start | bytes 207368 | tf_op jit(solution)/shard_map/ppermute | solution.py:506
  53.0 2.6 %collective-permute-start.7 = (f32[72,128]{1,0:T(8,128)S(1)}, f32[72,128]{1,0:T(8,128)S(1)}, u32[]{:S(2)}, u32[]{:S(2)}) collective-permute-start(f32[72,128]{1,0:T(8,128)S(1)} %get-tuple-element.48.near_ref), channel_id=1, source_target_pairs={{1,2},{2,1},{3,4},{4,3},{5,6},{6,5},{7,8},{8,7},{9,10},{10,9},{11,... | collective-permute-start | bytes 110600 | tf_op jit(solution)/shard_map/ppermute | solution.py:507
  53.7 3.1 %collective-permute-start.6 = (f32[72,128]{1,0:T(8,128)S(1)}, f32[72,128]{1,0:T(8,128)S(1)}, u32[]{:S(2)}, u32[]{:S(2)}) collective-permute-start(f32[72,128]{1,0:T(8,128)S(1)} %get-tuple-element.48.near_ref), channel_id=1, source_target_pairs={{0,1},{1,0},{2,3},{3,2},{4,5},{5,4},{6,7},{7,6},{8,9},{9,8},{10,11... | collective-permute-start | bytes 110600 | tf_op jit(solution)/shard_map/ppermute | solution.py:508
  56.9 10.7 %collective-permute-start.8 = (f32[72,128]{1,0:T(8,128)S(1)}, f32[72,128]{1,0:T(8,128)S(1)}, u32[]{:S(2)}, u32[]{:S(2)}) collective-permute-start(f32[72,128]{1,0:T(8,128)S(1)} %shard_map.135), channel_id=1, source_target_pairs={{0,32},{1,33},{2,34},{3,35},{4,36},{5,37},{6,38},{7,39},{8,40},{9,... | collective-permute-start | bytes 110600 | tf_op jit(solution)/shard_map/ppermute | solution.py:525
  62.4 14.4 %all-to-all-start.1 = ((f32[4,135,128]{2,1,0:T(8,128)}), f32[4,135,128]{2,1,0:T(8,128)S(1)}, u32[]{:S(2)}, u32[]{:S(2)}) async-start(f32[4,135,128]{2,1,0:T(8,128)} %shard_map.136), calls=%async_computation.1 | async-start | bytes 557056 | tf_op jit(solution)/shard_map/all_to_all | solution.py:569
  67.7 9.2 %collective-permute-start.9 = (f32[72,128]{1,0:T(8,128)S(1)}, f32[72,128]{1,0:T(8,128)S(1)}, u32[]{:S(2)}, u32[]{:S(2)}) collective-permute-start(f32[72,128]{1,0:T(8,128)S(1)} %shard_map.137), channel_id=1, source_target_pairs={{0,31},{31,0},{32,63},{63,32},{64,95},{95,64},{96,127},{127,96},{1... | collective-permute-start | bytes 110600 | tf_op jit(solution)/shard_map/ppermute | solution.py:544
  (3 other events, 5.4 us)
